TPU v7x, 512 devices: a whole 4x4x16 slice. The times are simulated.
512 devices in a mesh: outer: 16 (over y, z_lo), inner: 8 (over x, core), tensor: 4 (over z_hi).
Axes of the slice: x: 4, y: 4, z: 16 (z_hi: 4, z_lo: 4; z = z_hi * 4 + z_lo), core: 2. Of those that a mesh axis runs over, the one named last changes fastest.
Arguments:
- tokens: bfloat16 [16384, 8192], P(('outer', 'inner', 'tensor')), may hold values from -24 to 24
- ref_codes: bfloat16 [64, 128, 1024], P('inner', None, 'tensor'), may hold values from -4 to 4
- ref_scales: float32 [64, 1024], P('inner', 'tensor'), may hold values from 0.004 to 0.04
- policy_weight: bfloat16 [8192, 1024], P('inner', 'tensor'), may hold values from -0.1875 to 0.1875
- grad_keys: bfloat16 [16384, 1024], P(('outer', 'inner'), 'tensor'), may hold values from -6 to 6
Outputs:
- ref_keys: bfloat16 [16384, 1024], P(('outer', 'inner'), 'tensor')
- grad_weight: float32 [8192, 1024], P(('outer', 'inner'), 'tensor')
- grad_tokens: bfloat16 [16384, 8192], P(('outer', 'inner', 'tensor'))
All inputs are finite; a program needn't handle non-finite values.
Results may differ from a plain program's by a relative error of at most 0.013.
Values may be sent and summed in bfloat16 or wider, within the bound.
A program may use at most 64 MiB of HBM per device.

v0:
```python
import jax
import jax.numpy as jnp
from jax import lax
from jax.sharding import PartitionSpec as P


def body(tokens, ref_codes, ref_scales, policy_weight, grad_keys):
    gathered = lax.all_gather(tokens, "tensor", axis=0, tiled=True)
    tok_rows = gathered.shape[0]
    width = gathered.shape[1]
    key_cols = grad_keys.shape[1]
    block_rows = ref_codes.shape[1]
    zeros_keys = jnp.zeros((tok_rows, key_cols), jnp.float32)
    running = zeros_keys
    start = jnp.int32(0)
    codes = lax.all_gather(ref_codes, "inner", axis=0, tiled=True)
    scales = lax.all_gather(ref_scales.astype(jnp.bfloat16), "inner", axis=0, tiled=True).astype(
        jnp.float32
    )
    count = codes.shape[0]
    step_blocks = min(count, 8)
    for first in range(0, count, step_blocks):
        add_columns = lax.dynamic_slice_in_dim(
            gathered, (start + first) * block_rows, step_blocks * block_rows, 1
        )
        add_columns = add_columns.reshape(tok_rows, step_blocks, block_rows)
        products = lax.dot_general(
            add_columns,
            codes[first : first + step_blocks],
            (((2,), (1,)), ((1,), (0,))),
            preferred_element_type=jnp.float32,
        )
        running = running + jnp.sum(products * scales[first : first + step_blocks, None, :], axis=0)
    ref_keys = running.astype(jnp.bfloat16)
    slice_width = width // 8
    term_parts = []
    for index in range(8):
        columns = gathered[:, index * slice_width : (index + 1) * slice_width]
        product = lax.dot_general(
            columns, grad_keys, (((0,), (0,)), ((), ())), preferred_element_type=jnp.float32
        )
        term_parts.append(product.astype(jnp.bfloat16))
    term = jnp.concatenate(term_parts, axis=0)
    outer_count = lax.axis_size("outer")
    inner_count = lax.axis_size("inner")
    total_tokens = outer_count * inner_count * tok_rows
    grad_scale = lax.rsqrt(jnp.float32(total_tokens))
    own_rows = width // (outer_count * inner_count)
    shaped = term.reshape(outer_count * inner_count, own_rows, key_cols)
    received = lax.all_to_all(shaped, ("outer", "inner"), split_axis=0, concat_axis=0, tiled=True)
    weight_sum = jnp.sum(received, axis=0, dtype=jnp.float32)
    grad_weight = weight_sum * grad_scale
    partial_value = lax.dot_general(
        grad_keys,
        lax.all_gather(policy_weight, "inner", axis=0, tiled=True),
        (((1,), (1,)), ((), ())),
        preferred_element_type=jnp.float32,
    )
    rounded = lax.optimization_barrier(partial_value.astype(jnp.bfloat16)).astype(jnp.float32)
    summed = lax.psum_scatter(
        rounded.astype(jnp.bfloat16), "tensor", scatter_dimension=0, tiled=True
    )
    return (ref_keys, grad_weight, summed)


def solution(mesh):
    return jax.shard_map(
        body,
        mesh=mesh,
        in_specs=(
            P(("outer", "inner", "tensor"), None),
            P("inner", None, "tensor"),
            P("inner", "tensor"),
            P("inner", "tensor"),
            P(("outer", "inner"), "tensor"),
        ),
        out_specs=(
            P(("outer", "inner"), "tensor"),
            P(("outer", "inner"), "tensor"),
            P(("outer", "inner", "tensor"), None),
        ),
        check_vma=False,
    )
```

profile of v0, /device:TPU:1, one launch (start us, length us, event | category | flops | bytes accessed | tf_op | source)
XLA Modules:
  0.0 330.8 jit_solution(10636140541189712442)
XLA Ops:
  7.2 0.0 copy-start
  7.2 0.0 all-gather.4.cloned.1.call-start
  7.2 0.7 all-gather.4.cloned.1.call-update
  7.9 0.0 all-gather.8.cloned.1.call-start
  8.0 0.7 all-gather.8.cloned.1.call-update
  8.7 103.0 %all-gather.4.cloned.1.call-done = bf16[128,8192]{1,0:T(8,128)(2,1)} async-done(((bf16[32,8192]{1,0:T(8,128)(2,1)}), bf16[128,8192]{1,0:T(8,128)(2,1)}) %all-gather.4.cloned.1.call-update) | async-done | bytes 2097168 | tf_op jit(solution)/shard_map/all_gather | solution.py:8
  111.7 0.0 copy-done
  111.7 0.0 copy-start.1
  111.7 1.4 fusion.7
  113.1 1.3 fusion.6
  114.4 1.3 fusion.5
  115.7 1.3 fusion.4
  117.0 1.3 fusion.3
  118.2 0.0 copy-done.1
  118.2 0.3 fusion.2
  118.6 0.3 fusion.1
  118.9 0.3 fusion
  119.2 0.0 copy-start.2
  119.2 2.0 copy-done.2
  121.2 8.5 %all-to-all-start = ((bf16[128,64,256]{2,1,0:T(8,128)(2,1)}), bf16[128,64,256]{2,1,0:T(8,128)(2,1)}, u32[]{:S(2)}, u32[]{:S(2)}) async-start(bf16[128,64,256]{2,1,0:T(8,128)(2,1)} %bitcast.27), calls=%async_computation | async-start | bytes 8388608 | tf_op jit(solution)/shard_map/all_to_all | solution.py:50
  129.7 0.0 all-gather.6.cloned.1.call-start
  129.8 0.7 all-gather.6.cloned.1.call-update
  130.4 0.0 copy-start.3
  130.5 0.0 reduce-scatter.2.cloned.1.call-start
  130.5 54.7 %all-gather.8.cloned.1.call-done = bf16[8192,256]{1,0:T(8,128)(2,1)} async-done(((bf16[1024,256]{1,0:T(8,128)(2,1)}), bf16[8192,256]{1,0:T(8,128)(2,1)}) %all-gather.8.cloned.1.call-update) | async-done | bytes 4194320 | tf_op jit(solution)/shard_map/all_gather | solution.py:55
  185.2 5.0 %convolution_convert_fusion = bf16[128,8192]{1,0:T(8,128)(2,1)} fusion(bf16[128,256]{1,0:T(8,128)(2,1)S(1)} %copy-done, bf16[8192,256]{1,0:T(8,128)(2,1)} %all-gather.8.cloned.1.call-done), kind=kOutput, calls=%fused_computation | convolution fusion | flops 537919488 | bytes 6356992 | tf_op jit(solution)/shard_map/dot_general | solution.py:53
  190.2 0.0 reduce-scatter.2.cloned.1.call-update
  190.3 0.0 copy-done.3
  190.3 12.9 %all_gather.14 = bf16[64,256]{1,0:T(8,128)(2,1)S(1)} all-gather(bf16[8,256]{1,0:T(8,128)(2,1)S(1)} %convert_element_type.41), channel_id=1, replica_groups=mesh['outer'=16,'inner'=8,'tensor'=4] {'inner'}, dimensions={0}, use_global_device_ids=true | all-gather | bytes 36864 | tf_op jit(solution)/shard_map/all_gather | solution.py:17
  203.2 1.1 fusion.32
  204.2 1.1 copy.43
  205.4 1.1 copy.44
  206.5 1.1 copy.45
  207.6 0.2 copy.46
  207.8 0.2 copy.47
  208.0 0.2 copy.48
  208.2 0.2 copy.41
  208.3 0.2 copy.42
  208.5 20.2 %all-gather.6.cloned.1.call-done = bf16[64,128,256]{2,1,0:T(8,128)(2,1)} async-done(((bf16[8,128,256]{2,1,0:T(8,128)(2,1)}), bf16[64,128,256]{2,1,0:T(8,128)(2,1)}) %all-gather.6.cloned.1.call-update) | async-done | bytes 4194320 | tf_op jit(solution)/shard_map/all_gather | solution.py:16
  228.7 0.0 copy-start.4
  228.7 1.5 fusion.10
  230.3 1.4 fusion.11
  231.7 1.4 fusion.12
  233.1 1.4 fusion.13
  234.5 0.0 copy-done.4
  234.5 0.4 fusion.14
  234.9 0.3 fusion.15
  235.2 0.4 fusion.8
  235.6 0.3 fusion.9
  235.9 0.7 add_convert_fusion
  236.6 0.0 all-to-all-done
  236.6 2.8 convert_reduce_fusion
  239.5 0.6 broadcast_multiply_fusion
  240.1 84.2 %reduce-scatter.2.cloned.1.call-done = bf16[32,8192]{1,0:T(8,128)(2,1)} async-done(((bf16[128,8192]{1,0:T(8,128)(2,1)}), bf16[32,8192]{1,0:T(8,128)(2,1)}) %reduce-scatter.2.cloned.1.call-update) | async-done | bytes 524304 | tf_op jit(solution)/shard_map/reduce_scatter | solution.py:60
  (2 shorter events, 0.0 us)
Async XLA Ops:
  7.2 104.5 %copy-start = (bf16[128,256]{1,0:T(8,128)(2,1)S(1)}, bf16[128,256]{1,0:T(8,128)(2,1)}, u32[]{:S(2)}) copy-start(bf16[128,256]{1,0:T(8,128)(2,1)} %param.9) | copy-start | bytes 196612
  7.2 104.5 %all-gather.4.cloned.1.call-start = ((), (), s32[]{:S(2)}) async-start(), calls=%async_computation.2 | async-start | bytes 2621440 | tf_op jit(solution)/shard_map/all_gather | solution.py:8
  7.9 177.3 %all-gather.8.cloned.1.call-start = ((), (), s32[]{:S(2)}) async-start(), calls=%async_computation.4 | async-start | bytes 4718592 | tf_op jit(solution)/shard_map/all_gather | solution.py:55
  111.7 6.6 %copy-start.1 = (bf16[128,8192]{1,0:T(8,128)(2,1)S(1)}, bf16[128,8192]{1,0:T(8,128)(2,1)}, u32[]{:S(2)}) copy-start(bf16[128,8192]{1,0:T(8,128)(2,1)} %all-gather.4.cloned.1.call-done) | copy-start | bytes 6291460
  119.2 2.0 copy-start.2
  121.2 115.4 %all-to-all-start = ((bf16[128,64,256]{2,1,0:T(8,128)(2,1)}), bf16[128,64,256]{2,1,0:T(8,128)(2,1)}, u32[]{:S(2)}, u32[]{:S(2)}) async-start(bf16[128,64,256]{2,1,0:T(8,128)(2,1)} %bitcast.27), calls=%async_computation | async-start | bytes 8388608 | tf_op jit(solution)/shard_map/all_to_all | solution.py:50
  129.7 99.0 %all-gather.6.cloned.1.call-start = ((), (), s32[]{:S(2)}) async-start(), calls=%async_computation.3 | async-start | bytes 4718592 | tf_op jit(solution)/shard_map/all_gather | solution.py:16
  130.4 59.8 %copy-start.3 = (f32[8,256]{1,0:T(8,128)S(1)}, f32[8,256]{1,0:T(8,128)}, u32[]{:S(2)}) copy-start(f32[8,256]{1,0:T(8,128)} %param.7) | copy-start | bytes 24580
  130.5 193.8 %reduce-scatter.2.cloned.1.call-start = ((), (), s32[]{:S(2)}) async-start(), calls=%async_computation.5 | async-start | bytes 2621440 | tf_op jit(solution)/shard_map/reduce_scatter | solution.py:60
  228.7 5.8 %copy-start.4 = (bf16[64,128,256]{2,1,0:T(8,128)(2,1)S(1)}, bf16[64,128,256]{2,1,0:T(8,128)(2,1)}, u32[]{:S(2)}) copy-start(bf16[64,128,256]{2,1,0:T(8,128)(2,1)} %all-gather.6.cloned.1.call-done) | copy-start | bytes 12582916
Sparse Core Ops, SparseCore 0:
  10.1 101.5 all-gather.3
  113.8 71.3 all-gather.7
  187.4 41.3 all-gather.5
  232.0 92.2 reduce-scatter.1
where the time goes:
time: 331 us
  waiting for transfers between devices  264 us (80%)
  matrix products  19.6 us (6%)
  between operations  14 us (4%)
  blocking collectives  12.9 us (4%)
  starting transfers between devices  8.66 us (3%)
  local copies, waits for them, and re-layouts  7.27 us (2%)
  other arithmetic  4.15 us (1%)
    all_gather x1, waiting for transfers between devices, body(): gathered = lax.all_gather(tokens, 'tensor', axis=0, tiled=True)  103 us
    reduce_scatter x1, waiting for transfers between devices, body(): lax.psum_scatter(rounded.astype(jnp.bfloat16), 'tensor', scatter_dimensio...  84.2 us
    all_gather x1, waiting for transfers between devices, body(): lax.all_gather(policy_weight, 'inner', axis=0, tiled=True)  54.7 us
    all_gather x1, waiting for transfers between devices, body(): codes = lax.all_gather(ref_codes, 'inner', axis=0, tiled=True)  20.2 us
    all_gather x1, blocking collectives, body(): lax.all_gather(ref_scales.astype(jnp.bfloat16), 'inner', axis=0, tiled=True)  12.9 us
    all_to_all x1, starting transfers between devices, body(): lax.all_to_all(shaped, ('outer', 'inner'), split_axis=0, concat_axis=0, t...  8.51 us
    dot_general x8, matrix products, body(): lax.dot_general(columns, grad_keys, (((0,), (0,)), ((), ())), preferred_e...  7.48 us
    unnamed x19, local copies, waits for them, and re-layouts  7.27 us
  transfers between devices with their start and end apart: 5, of which 4 were waited for; matrix products, arithmetic and copies ran while one was open for 9% of the time, Pallas kernels for 0%

commit v1 on v0

v1 whole, which is shorter than its diff:
```python
import jax
import jax.numpy as jnp
from jax import lax
from jax.experimental import pallas as pl
from jax.experimental.pallas import tpu as pltpu
from jax.sharding import PartitionSpec as P

MESH = pl.DeviceIdType.MESH
F32 = jnp.float32
BF16 = jnp.bfloat16


def remote(src, dst, send_sem, recv_sem, device):
    return pltpu.make_async_remote_copy(
        src_ref=src,
        dst_ref=dst,
        send_sem=send_sem,
        recv_sem=recv_sem,
        device_id=device,
        device_id_type=MESH,
    )


def kernel(
    tok, codes, scales, policy, gkeys,
    keys_out, gw_out, gt_out,
    strips, slab, gk, cw_stage, cw, refs, sib, rs_own, rs, keys_part,
    xt, gwp, gw_send, gw_recv, gw_fin, gt_send, gt_recv,
    tok_s, tok_r, gkz_s, gkz_r, gk_s, gk_r, cwt_s, cwt_r, cw_s, cw_r,
    sib_s, sib_r, rs_s, rs_r, kz_s, kz_r, gw_s, gw_r, gwf_s, gwf_r, gt_s, gt_r,
):
    o = lax.axis_index("outer")
    i = lax.axis_index("inner")
    t = lax.axis_index("tensor")
    y, l = o // 4, o % 4
    x, c = i // 2, i % 2
    chip = y * 4 + x
    me = c * 16 + chip
    z = t * 4 + l

    def plane(p):
        return (((p % 16) // 4) * 4 + l, (p % 4) * 2 + p // 16, t)

    def at_z(zz):
        return (y * 4 + zz % 4, i, zz // 4)

    def at_chip(yy, xx):
        return (yy * 4 + l, xx * 2 + c, t)

    sibling = (o, x * 2 + (1 - c), t)
    up = at_z((z + 1) % 16)
    down = at_z((z + 15) % 16)

    barrier = pltpu.get_barrier_semaphore()

    @pl.loop(1, 32)
    def _(s):
        pl.semaphore_signal(barrier, inc=1, device_id=plane((me + s) % 32), device_id_type=MESH)

    for s in range(1, 4):
        pl.semaphore_signal(barrier, inc=1, device_id=(o, i, (t + s) % 4), device_id_type=MESH)
    pl.semaphore_signal(barrier, inc=1, device_id=up, device_id_type=MESH)
    pl.semaphore_signal(barrier, inc=1, device_id=down, device_id_type=MESH)

    for h in range(2):
        scale = scales[pl.ds(h * 4 + y, 1), :]
        cw_stage[h] = (codes[h * 4 + y].astype(F32) * scale).astype(BF16)
        cw_stage[2 + h] = policy[pl.ds(pl.multiple_of(h * 512 + y * 128, 128), 128), :]
    for p in range(32):
        pc, py, px = p // 16, (p % 16) // 4, p % 4
        for h in range(2):
            col = py * 2048 + (2 * pc + h) * 512 + px * 128
            strips[p, h] = tok[:, col : col + 128]
    slab[me] = strips[me]
    gk[me, t] = gkeys[pl.ds(pl.multiple_of(t * 32, 32), 32), :]

    pl.semaphore_wait(barrier, 36)

    for s in range(1, 4):
        tt = (t + s) % 4
        remote(
            gkeys.at[pl.ds(pl.multiple_of(tt * 32, 32), 32)], gk.at[me, t], gkz_s, gkz_r, (o, i, tt)
        ).start()

    @pl.when(x == y)
    def _():
        for k in range(4):
            cw[t * 4 + k] = cw_stage[k]

    @pl.when(x != y)
    def _():
        for k in range(4):
            remote(cw_stage.at[k], cw.at[t * 4 + k], cwt_s, cwt_r.at[k], at_chip(x, y)).start()

    @pl.loop(1, 32)
    def _(s):
        p = (me + s) % 32
        remote(strips.at[p], slab.at[me], tok_s, tok_r, plane(p)).start()

    remote(gk.at[me, pl.ds(0, 3)], gk.at[me, pl.ds(0, 3)], gkz_s, gkz_r, sibling).wait_recv()

    def a_chip(s):
        return (y + s * c) % 4, (x + s * (1 - c)) % 4

    def b_chip(s):
        return (y + s * (1 - c)) % 4, (x + s * c) % 4

    def gk_send(p, device):
        remote(gk.at[p], gk.at[p], gk_s, gk_r.at[p], device).start()

    def gk_wait(p):
        remote(gk.at[p], gk.at[p], gk_s, gk_r.at[p], sibling).wait_recv()

    for s in range(1, 4):
        gk_send(me, at_chip(*a_chip(s)))
    for s in range(1, 4):
        gk_send(me, at_chip(*b_chip(s)))
    gk_send(me, sibling)

    def cw_to(dirn, m, block, chunk, device):
        k = block * 4 + chunk
        remote(cw.at[k], cw.at[k], cw_s.at[dirn], cw_r.at[dirn, m], device).start()

    for k in range(4):
        @pl.when(x != y)
        def _():
            remote(cw.at[t * 4 + k], cw.at[t * 4 + k], cwt_s, cwt_r.at[k], sibling).wait_recv()

        @pl.when(l == 3)
        def _():
            cw_to(0, k, t, k, up)

        @pl.when(l == 0)
        def _():
            cw_to(1, k, t, k, down)

    def cw_step(m):
        ublock = (t + 3) % 4 if m < 4 else (t + 2) % 4
        uchunk = m if m < 4 else (0, 2)[m - 4]
        dblock = (t + 1) % 4 if m < 4 else (t + 2) % 4
        dchunk = m if m < 4 else (1, 3)[m - 4]
        ku = ublock * 4 + uchunk
        kd = dblock * 4 + dchunk
        remote(cw.at[ku], cw.at[ku], cw_s.at[0], cw_r.at[0, m], up).wait_recv()

        @pl.when(l < 3)
        def _():
            cw_to(0, m, ublock, uchunk, up)

        if m in (0, 2):
            @pl.when(l == 3)
            def _():
                cw_to(0, 4 + m // 2, ublock, uchunk, up)

        remote(cw.at[kd], cw.at[kd], cw_s.at[1], cw_r.at[1, m], down).wait_recv()

        @pl.when(l > 0)
        def _():
            cw_to(1, m, dblock, dchunk, down)

        if m in (1, 3):
            @pl.when(l == 0)
            def _():
                cw_to(1, 4 + m // 2, dblock, dchunk, down)

    def piece(a, b):
        yy = (y + a * c + b * (1 - c)) % 4
        xx = (x + a * (1 - c) + b * c) % 4
        return c * 16 + yy * 4 + xx

    cw_step(0)
    for a in range(1, 4):
        p = piece(a, 0)
        gk_wait(p)
        for s in range(1, 4):
            gk_send(p, at_chip(*b_chip(s)))
        gk_send(p, sibling)
    cw_step(1)
    for a in range(0, 4):
        for b in range(1, 4):
            p = piece(a, b)
            gk_wait(p)
            gk_send(p, sibling)
        if a == 1:
            cw_step(2)
    cw_step(3)

    remote(slab.at[pl.ds(0, 31)], slab.at[pl.ds(0, 31)], tok_s, tok_r, sibling).wait_recv()
    for h in range(2):
        xt[pl.ds(h * 128, 128), :] = slab[:, h].reshape(1024, 128).T

    for k in range(16):
        gk_wait((1 - c) * 16 + k)

    @pl.loop(0, 4)
    def _(tt):
        g = gk[:, tt].reshape(1024, 256)
        part = jnp.dot(xt[...], g, preferred_element_type=F32)
        gwp[tt * 2] = part[:128]
        gwp[tt * 2 + 1] = part[128:]

    def chain(dirn, d):
        zz = (z + d) % 16 if dirn == 0 else (z + 16 - d) % 16
        first = 8 if dirn == 0 else 7
        slot = (zz // 4) * 2 + zz % 2

        @pl.when((zz % 4) // 2 == c)
        def _():
            if d == first:
                gw_send[dirn, slot] = gwp[slot].astype(BF16)
            else:
                remote(
                    gw_recv.at[dirn, slot], gw_recv.at[dirn, slot], gw_s.at[dirn, slot], gw_r.at[dirn, slot], up
                ).wait_recv()
                gw_send[dirn, slot] = (gwp[slot] + gw_recv[dirn, slot].astype(F32)).astype(BF16)
            remote(
                gw_send.at[dirn, slot], gw_recv.at[dirn, slot], gw_s.at[dirn, slot], gw_r.at[dirn, slot],
                up if dirn == 0 else down,
            ).start()

    def chains(d):
        chain(0, d)
        if d < 8:
            chain(1, d)

    chains(8)
    cw_step(4)
    chains(7)
    cw_step(5)

    def code_of(tt):
        return jnp.concatenate([cw[tt * 4], cw[tt * 4 + 1]], axis=0)

    def rows_of(first):
        s = slab[pl.ds(first, 16)]
        return jnp.concatenate([s[:, 0].reshape(512, 128), s[:, 1].reshape(512, 128)], axis=1)

    @pl.loop(0, 4)
    def _(tt):
        part = jnp.dot(rows_of((1 - c) * 16), code_of(tt), preferred_element_type=F32)
        refs[tt] = part.astype(BF16).reshape(16, 32, 256)
        remote(refs.at[tt], sib.at[tt], sib_s, sib_r.at[tt], sibling).start()

    chains(6)

    @pl.loop(0, 4)
    def _(j):
        acc = jnp.zeros((256, 256), F32)
        for tt in range(4):
            g = gk[pl.ds(j * 8, 8), tt].reshape(256, 256)
            w = jnp.concatenate([cw[tt * 4 + 2], cw[tt * 4 + 3]], axis=0)
            acc = acc + lax.dot_general(g, w, (((1,), (1,)), ((), ())), preferred_element_type=F32)
        out = acc.astype(BF16)
        for h in range(2):
            gt_send[pl.ds(j * 8, 8), h] = out[:, h * 128 : (h + 1) * 128].reshape(8, 32, 128)

    gt_recv[me] = gt_send[me]

    @pl.loop(1, 32)
    def _(s):
        p = (me + s) % 32
        remote(gt_send.at[p], gt_recv.at[me], gt_s, gt_r, plane(p)).start()

    chains(5)

    @pl.loop(0, 4)
    def _(tt):
        part = jnp.dot(rows_of(c * 16), code_of(tt), preferred_element_type=F32)
        remote(sib.at[tt], sib.at[tt], sib_s, sib_r.at[tt], sibling).wait_recv()
        total = part.reshape(16, 32, 256) + sib[tt].astype(F32)
        rs_own[:, tt] = total.astype(BF16)

    rs[chip] = rs_own[chip]

    @pl.loop(1, 16)
    def _(s):
        k = (chip + s) % 16
        remote(rs_own.at[k], rs.at[chip], rs_s, rs_r, at_chip(k // 4, k % 4)).start()

    for d in (4, 3, 2, 1):
        chains(d)

    @pl.when(l // 2 == c)
    def _():
        slot = t * 2 + l % 2
        for dirn in range(2):
            remote(
                gw_recv.at[dirn, slot], gw_recv.at[dirn, slot], gw_s.at[dirn, slot], gw_r.at[dirn, slot], up
            ).wait_recv()
        total = gwp[slot] + gw_recv[0, slot].astype(F32) + gw_recv[1, slot].astype(F32)
        total = total * lax.rsqrt(jnp.full((1, 1), 16384.0, F32))
        gw_fin[0] = total[:64]
        gw_fin[1] = total[64:]
        remote(gw_fin.at[1 - c], gw_out, gwf_s, gwf_r, sibling).start()
        gw_out[...] = gw_fin[c]

    remote(rs.at[pl.ds(0, 15)], rs.at[pl.ds(0, 15)], rs_s, rs_r, sibling).wait_recv()
    for tt in range(4):
        acc = rs[0, tt].astype(F32)
        for k in range(1, 16):
            acc = acc + rs[k, tt].astype(F32)
        keys_part[tt] = acc.astype(BF16)
    mine = pl.ds(pl.multiple_of(t * 32, 32), 32)
    keys_out[mine, :] = keys_part[t]
    for s in range(1, 4):
        tt = (t + s) % 4
        remote(keys_part.at[tt], keys_out.at[mine], kz_s, kz_r, (o, i, tt)).start()

    remote(gt_recv.at[pl.ds(0, 31)], gt_recv.at[pl.ds(0, 31)], gt_s, gt_r, sibling).wait_recv()
    for p in range(32):
        pc, py, px = p // 16, (p % 16) // 4, p % 4
        for h in range(2):
            col = py * 2048 + (2 * pc + h) * 512 + px * 128
            gt_out[:, col : col + 128] = gt_recv[p, h]

    @pl.when(l // 2 != c)
    def _():
        remote(gw_fin.at[0], gw_out, gwf_s, gwf_r, sibling).wait_recv()

    @pl.when(l // 2 == c)
    def _():
        remote(gw_fin.at[0], gw_out, gwf_s, gwf_r, sibling).wait_send()

    remote(keys_out.at[pl.ds(0, 96)], keys_out.at[pl.ds(0, 96)], kz_s, kz_r, sibling).wait()
    remote(gkeys.at[pl.ds(0, 96)], gkeys.at[pl.ds(0, 96)], gkz_s, gkz_r, sibling).wait_send()
    remote(strips.at[pl.ds(0, 31)], strips.at[pl.ds(0, 31)], tok_s, tok_r, sibling).wait_send()
    remote(gk.at[pl.ds(0, 31)], gk.at[pl.ds(0, 31)], gk_s, gk_r.at[0], sibling).wait_send()

    @pl.when(x != y)
    def _():
        remote(cw_stage, cw_stage, cwt_s, cwt_r.at[0], sibling).wait_send()

    for dirn in range(2):
        remote(cw.at[pl.ds(0, 6)], cw.at[pl.ds(0, 6)], cw_s.at[dirn], cw_r.at[dirn, 0], sibling).wait_send()
    remote(refs, refs, sib_s, sib_r.at[0], sibling).wait_send()
    remote(rs_own.at[pl.ds(0, 15)], rs_own.at[pl.ds(0, 15)], rs_s, rs_r, sibling).wait_send()
    remote(gt_send.at[pl.ds(0, 31)], gt_send.at[pl.ds(0, 31)], gt_s, gt_r, sibling).wait_send()
    for dirn in range(2):
        for d in range(1, 9 if dirn == 0 else 8):
            zz = (z + d) % 16 if dirn == 0 else (z + 16 - d) % 16
            slot = (zz // 4) * 2 + zz % 2

            @pl.when((zz % 4) // 2 == c)
            def _():
                remote(
                    gw_send.at[dirn, slot], gw_send.at[dirn, slot], gw_s.at[dirn, slot], gw_r.at[dirn, slot], up
                ).wait_send()


def body(tokens, ref_codes, ref_scales, policy_weight, grad_keys):
    vmem = pl.BlockSpec(memory_space=pltpu.VMEM)
    dma = pltpu.SemaphoreType.DMA
    return pl.pallas_call(
        kernel,
        out_shape=(
            jax.ShapeDtypeStruct((128, 256), BF16),
            jax.ShapeDtypeStruct((64, 256), F32),
            jax.ShapeDtypeStruct((32, 8192), BF16),
        ),
        in_specs=[vmem] * 5,
        out_specs=[vmem] * 3,
        scratch_shapes=[
            pltpu.VMEM((32, 2, 32, 128), BF16),
            pltpu.VMEM((32, 2, 32, 128), BF16),
            pltpu.VMEM((32, 4, 32, 256), BF16),
            pltpu.VMEM((4, 128, 256), BF16),
            pltpu.VMEM((16, 128, 256), BF16),
            pltpu.VMEM((4, 16, 32, 256), BF16),
            pltpu.VMEM((4, 16, 32, 256), BF16),
            pltpu.VMEM((16, 4, 32, 256), BF16),
            pltpu.VMEM((16, 4, 32, 256), BF16),
            pltpu.VMEM((4, 32, 256), BF16),
            pltpu.VMEM((256, 1024), BF16),
            pltpu.VMEM((8, 128, 256), F32),
            pltpu.VMEM((2, 8, 128, 256), BF16),
            pltpu.VMEM((2, 8, 128, 256), BF16),
            pltpu.VMEM((2, 64, 256), F32),
            pltpu.VMEM((32, 2, 32, 128), BF16),
            pltpu.VMEM((32, 2, 32, 128), BF16),
            dma, dma, dma, dma,
            dma, dma((32,)),
            dma, dma((4,)),
            dma((2,)), dma((2, 6)),
            dma, dma((4,)),
            dma, dma, dma, dma,
            dma((2, 8)), dma((2, 8)),
            dma, dma, dma, dma,
        ],
        compiler_params=pltpu.CompilerParams(
            collective_id=0, has_side_effects=True, vmem_limit_bytes=48 * 1024 * 1024
        ),
        cost_estimate=pl.CostEstimate(flops=1_700_000_000, bytes_accessed=4_000_000, transcendentals=0),
    )(tokens, ref_codes, ref_scales, policy_weight, grad_keys)


def solution(mesh):
    return jax.shard_map(
        body,
        mesh=mesh,
        in_specs=(
            P(("outer", "inner", "tensor"), None),
            P("inner", None, "tensor"),
            P("inner", "tensor"),
            P("inner", "tensor"),
            P(("outer", "inner"), "tensor"),
        ),
        out_specs=(
            P(("outer", "inner"), "tensor"),
            P(("outer", "inner"), "tensor"),
            P(("outer", "inner", "tensor"), None),
        ),
        check_vma=False,
    )
```

time: 331 us -> 192 us (0.58)
  the two profiles are of different devices: /device:TPU:1 before, /device:TPU:38 now
where the time goes in v1:
time: 192 us
  Pallas kernels  185 us (96%)
  local copies, waits for them, and re-layouts  6.71 us (3%)
    pallas_call x1, Pallas kernels, body(): pl.pallas_call(kernel, out_shape=(jax.ShapeDtypeStruct((128, 256), BF16),...  185 us
    unnamed x13, local copies, waits for them, and re-layouts  6.71 us

profile of v1, /device:TPU:38, one launch (start us, length us, event | category | flops | bytes accessed | tf_op | source)
XLA Modules:
  0.0 192.0 jit_solution(9421824510040157804)
XLA Ops:
  0.6 0.0 copy-start
  0.6 1.0 copy-done
  1.7 0.0 copy-start.1
  1.7 1.0 copy-done.1
  2.7 0.0 copy-start.2
  2.7 1.0 copy-done.2
  3.8 0.0 copy-start.3
  3.8 0.8 copy-done.3
  4.6 0.0 copy-start.4
  4.6 0.7 copy-done.4
  5.3 184.6 %shard_map.76 = (bf16[128,256]{1,0:T(8,128)(2,1)S(1)}, f32[64,256]{1,0:T(8,128)S(1)}, bf16[32,8192]{1,0:T(8,128)(2,1)S(1)}) custom-call(bf16[32,8192]{1,0:T(8,128)(2,1)S(1)} %copy-done, bf16[8,128,256]{2,1,0:T(8,128)(2,1)S(1)} %copy-done.1, f32[8,256]{1,0:T(8,128)S(1)} %copy-done.4, bf16[1024,256]{1,0:T(8,128)(2,1)S(1)} %copy-done.2, ...), custom_call_target="tpu_custom_call" | custom-call | flops 1700000000 | bytes 4000000 | tf_op jit(solution)/shard_map/pallas_call | solution.py:353
  189.9 0.6 copy.11
  190.6 0.6 copy.12
  191.2 0.8 copy.13
Async XLA Ops:
  0.6 1.0 copy-start
  1.7 1.0 copy-start.1
  2.7 1.0 copy-start.2
  3.8 0.8 copy-start.3
  4.6 0.7 copy-start.4

commit v2 on v0

v2 whole, which is shorter than its diff:
```python
import jax
import jax.numpy as jnp
from jax import lax
from jax.experimental import pallas as pl
from jax.experimental.pallas import tpu as pltpu
from jax.sharding import PartitionSpec as P

MESH = pl.DeviceIdType.MESH
F32 = jnp.float32
BF16 = jnp.bfloat16


def remote(src, dst, send_sem, recv_sem, device):
    return pltpu.make_async_remote_copy(
        src_ref=src,
        dst_ref=dst,
        send_sem=send_sem,
        recv_sem=recv_sem,
        device_id=device,
        device_id_type=MESH,
    )


def among(value, *choices):
    found = value == choices[0]
    for choice in choices[1:]:
        found = found | (value == choice)
    return found


def kernel(
    tok, codes, scales, policy, gkeys,
    keys_out, gw_out, gt_out,
    codes_v, scales_v, gkeys_v, slab, gk, cw, xt, part, rs1, rs1_own, rs2, keys_part,
    gwx, gwx_send, gwx_recv, gwp, gw_send, gw_a, gw_b, gw_fin, gt_send,
    load_s, tok_s, tok_r, gkz_s, gkz_r, gk1_s, gk1_r, gk2_s, gk2_r, cw_s, cw_r, cws_s, cws_r,
    rs1_s, rs1_r, rs2_s, rs2_r, kz_s, kz_r, gwx_s, gwx_r, gw_s, gwa_r, gwb_r, fin_r, gt_s, gt_r,
):
    o = lax.axis_index("outer")
    i = lax.axis_index("inner")
    t = lax.axis_index("tensor")
    y, l = o // 4, o % 4
    x, c = i // 2, i % 2
    z = t * 4 + l
    a = jnp.where(c == 0, x, y)
    b = jnp.where(c == 0, y, x)
    me = a * 4 + b

    def place(aa, bb):
        yy = jnp.where(c == 0, bb, aa)
        xx = jnp.where(c == 0, aa, bb)
        return yy, xx

    def plane(aa, bb):
        yy, xx = place(aa, bb)
        return (yy * 4 + l, xx * 2 + c, t)

    def at_z(zz):
        return (y * 4 + zz % 4, i, zz // 4)

    sibling = (o, x * 2 + (1 - c), t)

    own_l = 2 * c + y // 2

    def final_device(tt, j):
        return (x * 4 + own_l, (2 * (y % 2) + j // 2) * 2 + j % 2, tt)

    def tree_place(tt):
        return (tt * 4 + own_l + 16 - z) % 16

    def is_final(d):
        return among(d, 0, 1, 5, 12, 15)

    def is_self(tt, j):
        fo, fi, ft = final_device(tt, j)
        return (fo == o) & (fi == i) & (ft == t)

    barrier = pltpu.get_barrier_semaphore()

    def greet(device):
        pl.semaphore_signal(barrier, inc=1, device_id=device, device_id_type=MESH)

    @pl.loop(1, 16)
    def _(s):
        k = (me + s) % 16
        greet(plane(k // 4, k % 4))

    greet(sibling)
    for dz in (1, 15, 2, 14, 4, 12, 8, 5, 11):
        greet(at_z((z + dz) % 16))
    src_y = 2 * (l % 2) + x // 2
    src_i = y * 2 + l // 2
    src_self = (src_y == y) & (src_i == i)
    for dz in (11, 15, 1, 4):
        zz = (z + dz) % 16
        greet((src_y * 4 + zz % 4, src_i, zz // 4))

    @pl.when(jnp.logical_not(src_self))
    def _():
        greet((src_y * 4 + l, src_i, t))

    greetings = jnp.int32(25)
    for tt in range(4):
        d = tree_place(tt)
        for j in range(4):
            counts = is_final(d) & jnp.logical_not(is_self(tt, j))
            greetings = greetings + jnp.where(counts, 1, 0)

    slice_cols = x * 2048 + y * 256
    loads = [
        pltpu.make_async_copy(gkeys, gkeys_v, load_s.at[0]),
        pltpu.make_async_copy(codes.at[pl.ds(2 * y, 2)], codes_v, load_s.at[1]),
        pltpu.make_async_copy(scales, scales_v, load_s.at[2]),
    ]
    for h in range(2):
        loads.append(
            pltpu.make_async_copy(
                policy.at[pl.ds(pl.multiple_of(y * 256 + h * 128, 128), 128)],
                cw.at[c * 16 + t * 4 + 2 + h],
                load_s.at[3 + h],
            )
        )
        loads.append(
            pltpu.make_async_copy(
                tok.at[:, pl.ds(pl.multiple_of(slice_cols + h * 1024, 256), 256)],
                slab.at[h, me],
                load_s.at[5 + h],
            )
        )
    for load in loads:
        load.start()
    for load in loads:
        load.wait()
    for h in range(2):
        cw[c * 16 + t * 4 + h] = (codes_v[h].astype(F32) * scales_v[pl.ds(2 * y + h, 1), :]).astype(BF16)
    gk[t, me] = gkeys_v[pl.ds(pl.multiple_of(t * 32, 32), 32), :]

    pl.semaphore_wait(barrier, greetings)

    def cw_copy(dirn, n, k, device):
        return remote(cw.at[k], cw.at[k], cw_s.at[dirn], cw_r.at[dirn, n], device)

    def cw_sibling(k):
        return remote(cw.at[k], cw.at[k], cws_s, cws_r.at[k % 16], sibling)

    own = c * 16 + t * 4
    for n, chunk in ((0, 0), (1, 1), (2, 0), (3, 2), (4, 3), (5, 2)):
        far = n in (2, 5)

        @pl.when(l == 3)
        def _():
            cw_copy(0, n, own + chunk, at_z((z + (5 if far else 1)) % 16)).start()

        @pl.when(l == 0)
        def _():
            cw_copy(1, n, own + chunk + (1 if far else 0), at_z((z + (11 if far else 15)) % 16)).start()

    for s in (2, 1, 3):
        tt = (t + s) % 4
        remote(
            gkeys_v.at[pl.ds(pl.multiple_of(tt * 32, 32), 32)], gk.at[t, me], gkz_s, gkz_r.at[s], (o, i, tt)
        ).start()

    def gk_first(tt):
        for s in range(1, 4):
            remote(gk.at[tt, me], gk.at[tt, me], gk1_s, gk1_r.at[tt, s], plane(a, (b + s) % 4)).start()

    def gk_second(tt):
        for s in range(1, 4):
            k = a * 4 + (b + 4 - s) % 4
            remote(gk.at[tt, k], gk.at[tt, k], gk1_s, gk1_r.at[tt, s], sibling).wait_recv()
        rows = gk.at[tt, pl.ds(a * 4, 4)]
        for s in range(1, 4):
            remote(rows, rows, gk2_s, gk2_r.at[tt, s], plane((a + s) % 4, b)).start()

    def gk_done(tt):
        for s in range(1, 4):
            rows = gk.at[tt, pl.ds((a + 4 - s) % 4 * 4, 4)]
            remote(rows, rows, gk2_s, gk2_r.at[tt, s], sibling).wait_recv()

    def gk_exchanged(s):
        tt = (t + 4 - s) % 4
        remote(gk.at[tt, me], gk.at[tt, me], gkz_s, gkz_r.at[s], sibling).wait_recv()
        gk_first(tt)

    gk_first(t)

    @pl.loop(1, 16)
    def _(s):
        k = (me + s) % 16
        yy, xx = place(k // 4, k % 4)
        for h in range(2):
            cols = pl.ds(pl.multiple_of(xx * 2048 + yy * 256 + h * 1024, 256), 256)
            remote(tok.at[:, cols], slab.at[h, me], tok_s, tok_r.at[h], plane(k // 4, k % 4)).start()

    for chunk in range(4):
        cw_sibling(own + chunk).start()

    def cw_step(dirn, n):
        far = n % 3 == 2
        third = n // 3
        chunk = jnp.where(far, 2 * third + dirn, n - third)
        step = jnp.where(far, 2, 1)
        block = (t + 4 - step) % 4 if dirn == 0 else (t + step) % 4
        k = c * 16 + block * 4 + chunk
        cw_copy(dirn, n, k, sibling).wait_recv()

        @pl.when((l < 3) if dirn == 0 else (l > 0))
        def _():
            cw_copy(dirn, n, k, at_z((z + (1 if dirn == 0 else 15)) % 16)).start()

        cw_sibling(k).start()

    def tick(s):
        n_up = s - 2 * l
        n_down = s - 2 * (3 - l)

        @pl.when((n_up >= 0) & (n_up < 6))
        def _():
            cw_step(0, n_up)

        @pl.when((n_down >= 0) & (n_down < 6))
        def _():
            cw_step(1, n_down)

    def codes_of(h, tt):
        k = h * 16 + tt * 4
        return jnp.concatenate([cw[k], cw[k + 1]], axis=0)

    def policy_of(h, tt):
        k = h * 16 + tt * 4 + 2
        return jnp.concatenate([cw[k], cw[k + 1]], axis=0)

    def sibling_chunks(tt, first):
        for chunk in (first, first + 1):
            k = (1 - c) * 16 + tt * 4 + chunk
            cw_sibling(k).wait_recv()

    def gw_part(tt):
        gk_done(tt)
        out = jnp.dot(xt[...], gk[tt].reshape(512, 256), preferred_element_type=F32)
        gwx[0] = out[:256]
        gwx[1] = out[256:]
        gwx_send[tt] = gwx[1 - c].astype(BF16)
        remote(gwx_send.at[tt], gwx_recv.at[tt], gwx_s, gwx_r.at[tt], sibling).start()
        gwp[tt] = gwx[c]

    def gw_first(tt):
        remote(gwx_send.at[tt], gwx_recv.at[tt], gwx_s, gwx_r.at[tt], sibling).wait_recv()
        gwp[tt] = gwp[tt] + gwx_recv[tt].astype(F32)
        d = tree_place(tt)
        down = among(d, 9, 11, 13)

        @pl.when(among(d, 2, 4, 6, 8) | down)
        def _():
            gw_send[tt] = gwp[tt].astype(BF16)
            remote(
                gw_send.at[tt], gw_a.at[tt], gw_s.at[tt, 4], gwa_r.at[tt], at_z((z + jnp.where(down, 15, 1)) % 16)
            ).start()

    def gw_add_a(tt):
        remote(gw_send.at[tt], gw_a.at[tt], gw_s.at[tt, 4], gwa_r.at[tt], sibling).wait_recv()
        gwp[tt] = gwp[tt] + gw_a[tt].astype(F32)

    def gw_second(tt):
        d = tree_place(tt)

        @pl.when(among(d, 3, 7, 10, 14))
        def _():
            gw_add_a(tt)
            gw_send[tt] = gwp[tt].astype(BF16)
            dz = jnp.where(d == 10, 14, jnp.where(d == 14, 15, 2))
            remote(gw_send.at[tt], gw_b.at[tt], gw_s.at[tt, 4], gwb_r.at[tt], at_z((z + dz) % 16)).start()

    def gw_third(tt):
        d = tree_place(tt)

        @pl.when(is_final(d))
        def _():
            @pl.when(among(d, 1, 5, 12))
            def _():
                gw_add_a(tt)

            @pl.when(among(d, 1, 5, 12, 15))
            def _():
                remote(gw_send.at[tt], gw_b.at[tt], gw_s.at[tt, 4], gwb_r.at[tt], sibling).wait_recv()
                gwp[tt] = gwp[tt] + gw_b[tt].astype(F32)

            gw_send[tt] = gwp[tt].astype(BF16)
            slot = jnp.where(d == 1, 1, jnp.where(d == 5, 2, jnp.where(d == 12, 3, jnp.where(d == 15, 4, 0))))
            for j in range(4):
                rows = gw_send.at[tt, pl.ds(j * 64, 64)]

                @pl.when(is_self(tt, j))
                def _():
                    gw_fin[0] = gw_send[tt, j * 64 : (j + 1) * 64]

                @pl.when(jnp.logical_not(is_self(tt, j)))
                def _():
                    remote(rows, gw_fin.at[slot], gw_s.at[tt, j], fin_r.at[slot], final_device(tt, j)).start()

    def ref_part(tt):
        out = jnp.dot(slab[0].reshape(512, 256), codes_of(0, tt), preferred_element_type=F32)
        out = out + jnp.dot(slab[1].reshape(512, 256), codes_of(1, tt), preferred_element_type=F32)
        part[tt] = out.astype(BF16).reshape(16, 32, 256)
        for s in range(1, 4):
            aa = (a + s) % 4
            remote(part.at[tt, pl.ds(aa * 4, 4)], rs1.at[tt, s - 1], rs1_s, rs1_r.at[tt, s], plane(aa, b)).start()

    def ref_second(tt):
        total = part[tt, pl.ds(a * 4, 4)].astype(F32)
        for s in range(1, 4):
            remote(rs1.at[tt, s - 1], rs1.at[tt, s - 1], rs1_s, rs1_r.at[tt, s], sibling).wait_recv()
            total = total + rs1[tt, s - 1].astype(F32)
        rs1_own[tt] = total.astype(BF16)
        for s in range(1, 4):
            bb = (b + s) % 4
            remote(rs1_own.at[tt, bb], rs2.at[tt, s - 1], rs2_s, rs2_r.at[tt, s], plane(a, bb)).start()

    mine = pl.ds(pl.multiple_of(t * 32, 32), 32)

    def ref_third(s):
        tt = (t + s) % 4
        total = rs1_own[tt, b].astype(F32)
        for q in range(1, 4):
            remote(rs2.at[tt, q - 1], rs2.at[tt, q - 1], rs2_s, rs2_r.at[tt, q], sibling).wait_recv()
            total = total + rs2[tt, q - 1].astype(F32)
        keys_part[tt] = total.astype(BF16)
        if s == 0:
            keys_out[mine, :] = keys_part[t]
        else:
            remote(keys_part.at[tt], keys_out.at[mine], kz_s, kz_r, (o, i, tt)).start()

    tick(0)
    gk_second(t)
    tick(1)
    gk_exchanged(1)
    gk_exchanged(3)
    tick(2)
    tick(3)
    gk_exchanged(2)
    gk_second((t + 3) % 4)
    gk_second((t + 1) % 4)
    tick(4)
    for h in range(2):
        remote(
            slab.at[h, pl.ds(0, 15)], slab.at[h, pl.ds(0, 15)], tok_s, tok_r.at[h], sibling
        ).wait_recv()
    for h in range(2):
        xt[pl.ds(h * 256, 256), :] = slab[h].reshape(512, 256).T
    gw_part(t)
    gk_second((t + 2) % 4)
    tick(5)
    sibling_chunks(t, 0)
    ref_part(t)
    tick(6)
    gw_part((t + 3) % 4)
    gw_part((t + 1) % 4)
    tick(7)
    for s in (3, 1):
        tt = (t + s) % 4
        sibling_chunks(tt, 0)
        ref_part(tt)
    tick(8)
    gw_part((t + 2) % 4)
    for s in (0, 3, 1):
        gw_first((t + s) % 4)
    tick(9)
    sibling_chunks((t + 2) % 4, 0)
    ref_part((t + 2) % 4)
    gw_first((t + 2) % 4)
    tick(10)
    ref_second(t)
    tick(11)
    for s in (3, 1):
        ref_second((t + s) % 4)

    for tt in range(4):
        sibling_chunks(tt, 2)

    @pl.loop(0, 2)
    def _(j):
        rows = [gk[tt, pl.ds(j * 8, 8)].reshape(256, 256) for tt in range(4)]
        for h in range(2):
            acc = jnp.zeros((256, 256), F32)
            for tt in range(4):
                acc = acc + lax.dot_general(
                    rows[tt], policy_of(h, tt), (((1,), (1,)), ((), ())), preferred_element_type=F32
                )
            gt_send[h, pl.ds(j * 8, 8)] = acc.astype(BF16).reshape(8, 32, 256)

    def gt_cols(h):
        return pl.ds(pl.multiple_of(slice_cols + h * 1024, 256), 256)

    @pl.loop(1, 16)
    def _(s):
        k = (me + s) % 16
        for h in range(2):
            remote(gt_send.at[h, k], gt_out.at[:, gt_cols(h)], gt_s, gt_r, plane(k // 4, k % 4)).start()

    gt_own = [pltpu.make_async_copy(gt_send.at[h, me], gt_out.at[:, gt_cols(h)], load_s.at[h]) for h in range(2)]
    for copy in gt_own:
        copy.start()

    for tt in range(4):
        gw_second(tt)
    ref_second((t + 2) % 4)
    for s in (0, 3, 1):
        ref_third(s)
    for tt in range(4):
        gw_third(tt)
    ref_third(2)

    total = jnp.zeros((64, 256), F32)
    for slot in range(5):
        def arrived():
            remote(gw_fin.at[slot], gw_fin.at[slot], gw_s.at[0, 0], fin_r.at[slot], sibling).wait_recv()

        if slot == 0:
            pl.when(jnp.logical_not(src_self))(arrived)
        else:
            arrived()
        total = total + gw_fin[slot].astype(F32)
    gw_out[...] = total * lax.rsqrt(jnp.full((1, 1), 16384.0, F32))

    for copy in gt_own:
        copy.wait()
    gt_all = gt_out.at[:, pl.ds(0, 30 * 256)]
    remote(gt_all, gt_all, gt_s, gt_r, sibling).wait_recv()
    remote(keys_out.at[pl.ds(0, 96)], keys_out.at[pl.ds(0, 96)], kz_s, kz_r, sibling).wait()
    remote(gkeys_v.at[pl.ds(0, 96)], gkeys_v.at[pl.ds(0, 96)], gkz_s, gkz_r.at[0], sibling).wait_send()
    remote(gt_all, gt_all, tok_s, tok_r.at[0], sibling).wait_send()
    remote(gt_all, gt_all, gt_s, gt_r, sibling).wait_send()
    remote(gk.at[0, pl.ds(0, 12)], gk.at[0, pl.ds(0, 12)], gk1_s, gk1_r.at[0, 0], sibling).wait_send()
    remote(gk.at[pl.ds(0, 3)], gk.at[pl.ds(0, 3)], gk2_s, gk2_r.at[0, 0], sibling).wait_send()
    remote(part.at[pl.ds(0, 3)], part.at[pl.ds(0, 3)], rs1_s, rs1_r.at[0, 0], sibling).wait_send()
    remote(rs2, rs2, rs2_s, rs2_r.at[0, 0], sibling).wait_send()
    for dirn in range(2):
        remote(cw.at[pl.ds(0, 6)], cw.at[pl.ds(0, 6)], cw_s.at[dirn], cw_r.at[dirn, 0], sibling).wait_send()
    remote(cw.at[pl.ds(0, 16)], cw.at[pl.ds(0, 16)], cws_s, cws_r.at[0], sibling).wait_send()
    remote(gwx_send, gwx_send, gwx_s, gwx_r.at[0], sibling).wait_send()
    for tt in range(4):
        final = is_final(tree_place(tt))

        @pl.when(jnp.logical_not(final))
        def _():
            remote(gw_send.at[tt], gw_send.at[tt], gw_s.at[tt, 4], gwa_r.at[tt], sibling).wait_send()

        for j in range(4):
            rows = gw_send.at[tt, pl.ds(j * 64, 64)]

            @pl.when(final & jnp.logical_not(is_self(tt, j)))
            def _():
                remote(rows, rows, gw_s.at[tt, j], gwa_r.at[tt], sibling).wait_send()


def body(tokens, ref_codes, ref_scales, policy_weight, grad_keys):
    vmem = pl.BlockSpec(memory_space=pltpu.VMEM)
    hbm = pl.BlockSpec(memory_space=pltpu.HBM)
    dma = pltpu.SemaphoreType.DMA
    return pl.pallas_call(
        kernel,
        out_shape=(
            jax.ShapeDtypeStruct((128, 256), BF16),
            jax.ShapeDtypeStruct((64, 256), F32),
            jax.ShapeDtypeStruct((32, 8192), BF16),
        ),
        in_specs=[hbm] * 5,
        out_specs=[vmem, vmem, hbm],
        scratch_shapes=[
            pltpu.VMEM((2, 128, 256), BF16),
            pltpu.VMEM((8, 256), F32),
            pltpu.VMEM((128, 256), BF16),
            pltpu.VMEM((2, 16, 32, 256), BF16),
            pltpu.VMEM((4, 16, 32, 256), BF16),
            pltpu.VMEM((32, 128, 256), BF16),
            pltpu.VMEM((512, 512), BF16),
            pltpu.VMEM((4, 16, 32, 256), BF16),
            pltpu.VMEM((4, 3, 4, 32, 256), BF16),
            pltpu.VMEM((4, 4, 32, 256), BF16),
            pltpu.VMEM((4, 3, 32, 256), BF16),
            pltpu.VMEM((4, 32, 256), BF16),
            pltpu.VMEM((2, 256, 256), F32),
            pltpu.VMEM((4, 256, 256), BF16),
            pltpu.VMEM((4, 256, 256), BF16),
            pltpu.VMEM((4, 256, 256), F32),
            pltpu.VMEM((4, 256, 256), BF16),
            pltpu.VMEM((4, 256, 256), BF16),
            pltpu.VMEM((4, 256, 256), BF16),
            pltpu.VMEM((5, 64, 256), BF16),
            pltpu.VMEM((2, 16, 32, 256), BF16),
            dma((7,)),
            dma, dma((2,)),
            dma, dma((4,)),
            dma, dma((4, 4)), dma, dma((4, 4)),
            dma((2,)), dma((2, 6)), dma, dma((16,)),
            dma, dma((4, 4)), dma, dma((4, 4)),
            dma, dma,
            dma, dma((4,)),
            dma((4, 5)), dma((4,)), dma((4,)), dma((5,)),
            dma, dma,
        ],
        compiler_params=pltpu.CompilerParams(
            collective_id=0, has_side_effects=True, vmem_limit_bytes=48 * 1024 * 1024
        ),
        cost_estimate=pl.CostEstimate(flops=1_700_000_000, bytes_accessed=4_000_000, transcendentals=0),
    )(tokens, ref_codes, ref_scales, policy_weight, grad_keys)


def solution(mesh):
    return jax.shard_map(
        body,
        mesh=mesh,
        in_specs=(
            P(("outer", "inner", "tensor"), None),
            P("inner", None, "tensor"),
            P("inner", "tensor"),
            P("inner", "tensor"),
            P(("outer", "inner"), "tensor"),
        ),
        out_specs=(
            P(("outer", "inner"), "tensor"),
            P(("outer", "inner"), "tensor"),
            P(("outer", "inner", "tensor"), None),
        ),
        check_vma=False,
    )
```

time: 331 us -> 84.9 us (0.26)
  the two profiles are of different devices: /device:TPU:1 before, /device:TPU:39 now
where the time goes in v2:
time: 84.9 us; the launch traced here: 84.5 us
  Pallas kernels  77.2 us (91%)
  local copies, waits for them, and re-layouts  6.71 us (8%)
    pallas_call x1, Pallas kernels, body(): pl.pallas_call(kernel, out_shape=(jax.ShapeDtypeStruct((128, 256), BF16),...  77.2 us
    unnamed x13, local copies, waits for them, and re-layouts  6.71 us

profile of v2, /device:TPU:39, one launch (start us, length us, event | category | flops | bytes accessed | tf_op | source)
XLA Modules:
  0.0 84.5 jit_solution(4908165938579709578)
XLA Ops:
  0.6 0.0 copy-start
  0.6 1.0 %copy-done = bf16[32,8192]{1,0:T(8,128)(2,1)S(1)} copy-done((bf16[32,8192]{1,0:T(8,128)(2,1)S(1)}, bf16[32,8192]{1,0:T(8,128)(2,1)}, u32[]{:S(2)}) %copy-start) | copy-done | bytes 524312
  1.7 0.0 copy-start.1
  1.7 1.0 %copy-done.1 = bf16[8,128,256]{2,1,0:T(8,128)(2,1)S(1)} copy-done((bf16[8,128,256]{2,1,0:T(8,128)(2,1)S(1)}, bf16[8,128,256]{2,1,0:T(8,128)(2,1)}, u32[]{:S(2)}) %copy-start.1) | copy-done | bytes 524312
  2.7 0.0 copy-start.2
  2.7 1.0 %copy-done.2 = bf16[1024,256]{1,0:T(8,128)(2,1)S(1)} copy-done((bf16[1024,256]{1,0:T(8,128)(2,1)S(1)}, bf16[1024,256]{1,0:T(8,128)(2,1)}, u32[]{:S(2)}) %copy-start.2) | copy-done | bytes 524312
  3.8 0.0 copy-start.3
  3.8 0.8 copy-done.3
  4.6 0.0 copy-start.4
  4.6 0.7 copy-done.4
  5.3 77.2 %shard_map.76 = (bf16[128,256]{1,0:T(8,128)(2,1)S(1)}, f32[64,256]{1,0:T(8,128)S(1)}, bf16[32,8192]{1,0:T(8,128)(2,1)S(1)}) custom-call(bf16[32,8192]{1,0:T(8,128)(2,1)S(1)} %copy-done, bf16[8,128,256]{2,1,0:T(8,128)(2,1)S(1)} %copy-done.1, f32[8,256]{1,0:T(8,128)S(1)} %copy-done.4, bf16[1024,256]{1,0:T(8,128)(2,1)S(1)} %copy-done.2, ...), custom_call_target="tpu_custom_call" | custom-call | flops 1700000000 | bytes 4000000 | tf_op jit(solution)/shard_map/pallas_call | solution.py:461
  82.5 0.6 copy.11
  83.1 0.6 copy.12
  83.7 0.8 copy.13
Async XLA Ops:
  0.6 1.0 %copy-start = (bf16[32,8192]{1,0:T(8,128)(2,1)S(1)}, bf16[32,8192]{1,0:T(8,128)(2,1)}, u32[]{:S(2)}) copy-start(bf16[32,8192]{1,0:T(8,128)(2,1)} %tok.1) | copy-start | bytes 1572868
  1.7 1.0 %copy-start.1 = (bf16[8,128,256]{2,1,0:T(8,128)(2,1)S(1)}, bf16[8,128,256]{2,1,0:T(8,128)(2,1)}, u32[]{:S(2)}) copy-start(bf16[8,128,256]{2,1,0:T(8,128)(2,1)} %codes.1) | copy-start | bytes 1572868
  2.7 1.0 %copy-start.2 = (bf16[1024,256]{1,0:T(8,128)(2,1)S(1)}, bf16[1024,256]{1,0:T(8,128)(2,1)}, u32[]{:S(2)}) copy-start(bf16[1024,256]{1,0:T(8,128)(2,1)} %policy.1) | copy-start | bytes 1572868
  3.8 0.8 copy-start.3
  4.6 0.7 copy-start.4

commit v3 on v2

v3 whole, which is shorter than its diff:
```python
import jax
import jax.numpy as jnp
from jax import lax
from jax.experimental import pallas as pl
from jax.experimental.pallas import tpu as pltpu
from jax.sharding import PartitionSpec as P

MESH = pl.DeviceIdType.MESH
F32 = jnp.float32
BF16 = jnp.bfloat16


CHUNKS = ((0, 1, 2, 3), (1, 0, 3, 2))
STARTS = (0, 2, 4, 7, 8, 13)


def remote(src, dst, send_sem, recv_sem, device):
    return pltpu.make_async_remote_copy(
        src_ref=src,
        dst_ref=dst,
        send_sem=send_sem,
        recv_sem=recv_sem,
        device_id=device,
        device_id_type=MESH,
    )


def among(value, *choices):
    found = value == choices[0]
    for choice in choices[1:]:
        found = found | (value == choice)
    return found


def kernel(
    tok, codes, scales, policy, gkeys,
    keys_out, gw_out, gt_out,
    codes_v, scales_v, gkeys_v, slab, gk, cw, xt, part, rs1, rs1_own, rs2, keys_part,
    gwx_send, gwx_recv, gwp, gw_send, gw_a, gw_b, gw_fin, gt_send,
    load_s, tok_s, tok_r, gkz_s, gkz_r, gk1_s, gk1_r, gk2_s, gk2_r, gkd_s, gkd_r, cw_s, cw_r, cws_s, cws_r,
    rs1_s, rs1_r, rs2_s, rs2_r, kz_s, kz_r, gwx_s, gwx_r, gw_s, gwa_r, gwb_r, fin_r, gt_s, gt_r,
    near_in, far_in,
):
    o = lax.axis_index("outer")
    i = lax.axis_index("inner")
    t = lax.axis_index("tensor")
    y, l = o // 4, o % 4
    x, c = i // 2, i % 2
    z = t * 4 + l
    a = jnp.where(c == 0, x, y)
    b = jnp.where(c == 0, y, x)
    me = a * 4 + b

    def place(aa, bb):
        yy = jnp.where(c == 0, bb, aa)
        xx = jnp.where(c == 0, aa, bb)
        return yy, xx

    def plane(aa, bb):
        yy, xx = place(aa, bb)
        return (yy * 4 + l, xx * 2 + c, t)

    def at_z(zz):
        return (y * 4 + zz % 4, i, zz // 4)

    sibling = (o, x * 2 + (1 - c), t)

    own_l = 2 * c + y // 2

    def final_device(tt, j):
        return (x * 4 + own_l, (2 * (y % 2) + j // 2) * 2 + j % 2, tt)

    def tree_place(tt, q):
        d = (tt * 4 + own_l + 16 - z) % 16
        return d if q == 0 else (16 - d) % 16

    def tree_device(dz, q):
        return at_z((z + (dz if q == 0 else 16 - dz)) % 16)

    def is_final(d):
        return among(d, 0, 1, 5, 12, 15)

    def is_self(tt, j):
        fo, fi, ft = final_device(tt, j)
        return (fo == o) & (fi == i) & (ft == t)

    barrier = pltpu.get_barrier_semaphore()

    def greet(device):
        pl.semaphore_signal(barrier, inc=1, device_id=device, device_id_type=MESH)

    @pl.loop(1, 16)
    def _(s):
        k = (me + s) % 16
        greet(plane(k // 4, k % 4))

    greet(sibling)
    for dz in (1, 15, 4, 12):
        greet(at_z((z + dz) % 16))

    slice_cols = x * 2048 + y * 256
    loads = [
        pltpu.make_async_copy(gkeys, gkeys_v, load_s.at[0]),
        pltpu.make_async_copy(codes.at[pl.ds(2 * y, 2)], codes_v, load_s.at[1]),
        pltpu.make_async_copy(scales, scales_v, load_s.at[2]),
    ]
    for h in range(2):
        loads.append(
            pltpu.make_async_copy(
                policy.at[pl.ds(pl.multiple_of(y * 256 + h * 128, 128), 128)],
                cw.at[c * 16 + t * 4 + 2 + h],
                load_s.at[3 + h],
            )
        )
        loads.append(
            pltpu.make_async_copy(
                tok.at[:, pl.ds(pl.multiple_of(slice_cols + h * 1024, 256), 256)],
                slab.at[h, me],
                load_s.at[5 + h],
            )
        )
    for load in loads:
        load.start()
    for load in loads:
        load.wait()
    for h in range(2):
        cw[c * 16 + t * 4 + h] = (codes_v[h].astype(F32) * scales_v[pl.ds(2 * y + h, 1), :]).astype(BF16)
    gk[t, me] = gkeys_v[pl.ds(pl.multiple_of(t * 32, 32), 32), :]

    pl.semaphore_wait(barrier, 20)

    def tell(sem, device):
        pl.semaphore_signal(sem, inc=1, device_id=device, device_id_type=MESH)

    tell(near_in, sibling)
    for dz in (1, 15, 4, 12):
        tell(near_in, at_z((z + dz) % 16))

    def heard_near():
        pl.semaphore_wait(near_in, 5)
        for dz in (1, 15, 4, 12, 5, 11):
            tell(far_in, at_z((z + dz) % 16))

    def heard_far():
        pl.semaphore_wait(far_in, 6)

    def cw_copy(dirn, n, k, device):
        return remote(cw.at[k], cw.at[k], cw_s.at[dirn], cw_r.at[dirn, n], device)

    def cw_sibling(k):
        return remote(cw.at[k], cw.at[k], cws_s, cws_r.at[k % 16], sibling)

    def gk_send(s):
        tt = (t + s) % 4
        remote(
            gkeys_v.at[pl.ds(pl.multiple_of(tt * 32, 32), 32)], gk.at[t, me], gkz_s, gkz_r.at[s], (o, i, tt)
        ).start()

    gk_send(1)
    gk_send(3)

    def gk_first(tt):
        for s in range(1, 4):
            remote(gk.at[tt, me], gk.at[tt, me], gk1_s, gk1_r.at[tt, s], plane(a, (b + s) % 4)).start()

    def gk_second(tt):
        for s in range(1, 4):
            k = a * 4 + (b + 4 - s) % 4
            remote(gk.at[tt, k], gk.at[tt, k], gk1_s, gk1_r.at[tt, s], sibling).wait_recv()
        rows = gk.at[tt, pl.ds(a * 4, 4)]
        for s in range(1, 4):
            remote(rows, rows, gk2_s, gk2_r.at[tt, s], plane((a + s) % 4, b)).start()

    def gk_done(tt, direct=False):
        if direct:
            rows = gk.at[tt, pl.ds(0, 15)]
            remote(rows, rows, gkd_s, gkd_r, sibling).wait_recv()
            return
        for s in range(1, 4):
            rows = gk.at[tt, pl.ds((a + 4 - s) % 4 * 4, 4)]
            remote(rows, rows, gk2_s, gk2_r.at[tt, s], sibling).wait_recv()

    def gk_direct(tt):
        @pl.loop(1, 16)
        def _(s):
            k = (me + s) % 16
            remote(gk.at[tt, me], gk.at[tt, me], gkd_s, gkd_r, plane(k // 4, k % 4)).start()

    def gk_exchanged(s):
        tt = (t + 4 - s) % 4
        remote(gk.at[tt, me], gk.at[tt, me], gkz_s, gkz_r.at[s], sibling).wait_recv()
        if s == 2:
            gk_direct(tt)
        else:
            gk_first(tt)

    gk_first(t)

    own = c * 16 + t * 4
    for n in range(4):
        @pl.when(l == 3)
        def _():
            cw_copy(0, n, own + CHUNKS[0][n], at_z((z + 1) % 16)).start()

        @pl.when(l == 0)
        def _():
            cw_copy(1, n, own + CHUNKS[1][n], at_z((z + 15) % 16)).start()

    @pl.loop(1, 16)
    def _(s):
        k = (me + s) % 16
        yy, xx = place(k // 4, k % 4)
        for h in range(2):
            cols = pl.ds(pl.multiple_of(xx * 2048 + yy * 256 + h * 1024, 256), 256)
            remote(tok.at[:, cols], slab.at[h, me], tok_s, tok_r.at[h], plane(k // 4, k % 4)).start()

    for chunk in range(4):
        cw_sibling(own + chunk).start()

    def cw_step(dirn, n, steps):
        far = n >= 4
        block = (t + (2 if far else 3 if dirn == 0 else 1)) % 4
        k = c * 16 + block * 4 + CHUNKS[dirn][2 * (n - 4) if far else n]
        onward = 1 if dirn == 0 else 15
        cw_copy(dirn, n, k, sibling).wait_recv()
        if steps < 3:
            cw_copy(dirn, n, k, at_z((z + onward) % 16)).start()
        if steps == 0 and n in (0, 2):
            cw_copy(dirn, 4 + n // 2, k, at_z((z + 4 * onward) % 16)).start()
        cw_sibling(k).start()

    def tick(s):
        for chip in range(4):
            for dirn, steps in ((0, chip), (1, 3 - chip)):
                for n, start in enumerate(STARTS):
                    if start + 5 * steps == s:
                        @pl.when(l == chip)
                        def _():
                            cw_step(dirn, n, steps)

    def codes_of(h, tt):
        k = h * 16 + tt * 4
        return jnp.concatenate([cw[k], cw[k + 1]], axis=0)

    def policy_of(h, tt):
        k = h * 16 + tt * 4 + 2
        return jnp.concatenate([cw[k], cw[k + 1]], axis=0)

    def sibling_chunks(tt, first):
        for chunk in (first, first + 1):
            k = (1 - c) * 16 + tt * 4 + chunk
            cw_sibling(k).wait_recv()

    def gw_part(s):
        tt = (t + s) % 4
        gk_done(tt, s == 2)
        g = gk[tt].reshape(512, 256)
        gwx_send[tt] = jnp.dot(xt[1 - c], g, preferred_element_type=F32).astype(BF16).reshape(2, 128, 256)
        remote(gwx_send.at[tt], gwx_recv.at[tt], gwx_s, gwx_r.at[tt], sibling).start()
        gwp[tt] = jnp.dot(xt[c], g, preferred_element_type=F32).reshape(2, 128, 256)

    def gw_first(tt):
        remote(gwx_send.at[tt], gwx_recv.at[tt], gwx_s, gwx_r.at[tt], sibling).wait_recv()
        for q in range(2):
            gwp[tt, q] = gwp[tt, q] + gwx_recv[tt, q].astype(F32)
            d = tree_place(tt, q)
            down = among(d, 9, 11, 13)

            @pl.when(among(d, 2, 4, 6, 8) | down)
            def _():
                gw_send[tt, q] = gwp[tt, q].astype(BF16)
                remote(
                    gw_send.at[tt, q], gw_a.at[tt, q], gw_s.at[tt, q, 2], gwa_r.at[tt, q],
                    tree_device(jnp.where(down, 15, 1), q),
                ).start()

    def gw_add_a(tt, q):
        remote(gw_send.at[tt, q], gw_a.at[tt, q], gw_s.at[tt, q, 2], gwa_r.at[tt, q], sibling).wait_recv()
        gwp[tt, q] = gwp[tt, q] + gw_a[tt, q].astype(F32)

    def gw_second(tt):
        for q in range(2):
            d = tree_place(tt, q)

            @pl.when(among(d, 3, 7, 10, 14))
            def _():
                gw_add_a(tt, q)
                gw_send[tt, q] = gwp[tt, q].astype(BF16)
                dz = jnp.where(d == 10, 14, jnp.where(d == 14, 15, 2))
                remote(
                    gw_send.at[tt, q], gw_b.at[tt, q], gw_s.at[tt, q, 2], gwb_r.at[tt, q], tree_device(dz, q)
                ).start()

    def gw_third(tt):
        for q in range(2):
            d = tree_place(tt, q)

            @pl.when(is_final(d))
            def _():
                @pl.when(among(d, 1, 5, 12))
                def _():
                    gw_add_a(tt, q)

                @pl.when(among(d, 1, 5, 12, 15))
                def _():
                    remote(
                        gw_send.at[tt, q], gw_b.at[tt, q], gw_s.at[tt, q, 2], gwb_r.at[tt, q], sibling
                    ).wait_recv()
                    gwp[tt, q] = gwp[tt, q] + gw_b[tt, q].astype(F32)

                gw_send[tt, q] = gwp[tt, q].astype(BF16)
                slot = jnp.where(d == 1, 1, jnp.where(d == 5, 2, jnp.where(d == 12, 3, jnp.where(d == 15, 4, 0))))
                for e in range(2):
                    j = 2 * q + e

                    @pl.when(is_self(tt, j))
                    def _():
                        gw_fin[0] = gw_send[tt, q, e * 64 : (e + 1) * 64]

                    @pl.when(jnp.logical_not(is_self(tt, j)))
                    def _():
                        remote(
                            gw_send.at[tt, q, pl.ds(e * 64, 64)], gw_fin.at[slot], gw_s.at[tt, q, e],
                            fin_r.at[slot], final_device(tt, j),
                        ).start()

    def ref_part(tt):
        rows = jnp.concatenate([slab[0].reshape(512, 256), slab[1].reshape(512, 256)], axis=1)
        both = jnp.concatenate([codes_of(0, tt), codes_of(1, tt)], axis=0)
        out = jnp.dot(rows, both, preferred_element_type=F32)
        part[tt] = out.astype(BF16).reshape(16, 32, 256)
        for s in range(1, 4):
            aa = (a + s) % 4
            remote(part.at[tt, pl.ds(aa * 4, 4)], rs1.at[tt, s - 1], rs1_s, rs1_r.at[tt, s], plane(aa, b)).start()

    def ref_second(tt):
        total = part[tt, pl.ds(a * 4, 4)].astype(F32)
        for s in range(1, 4):
            remote(rs1.at[tt, s - 1], rs1.at[tt, s - 1], rs1_s, rs1_r.at[tt, s], sibling).wait_recv()
            total = total + rs1[tt, s - 1].astype(F32)
        rs1_own[tt] = total.astype(BF16)
        for s in range(1, 4):
            bb = (b + s) % 4
            remote(rs1_own.at[tt, bb], rs2.at[tt, s - 1], rs2_s, rs2_r.at[tt, s], plane(a, bb)).start()

    mine = pl.ds(pl.multiple_of(t * 32, 32), 32)

    def ref_third(s):
        tt = (t + s) % 4
        total = rs1_own[tt, b].astype(F32)
        for q in range(1, 4):
            remote(rs2.at[tt, q - 1], rs2.at[tt, q - 1], rs2_s, rs2_r.at[tt, q], sibling).wait_recv()
            total = total + rs2[tt, q - 1].astype(F32)
        keys_part[tt] = total.astype(BF16)
        if isinstance(s, int) and s == 0:
            keys_out[mine, :] = keys_part[t]
        else:
            remote(keys_part.at[tt], keys_out.at[mine], kz_s, kz_r, (o, i, tt)).start()

    def tokens_done():
        for h in range(2):
            remote(
                slab.at[h, pl.ds(0, 15)], slab.at[h, pl.ds(0, 15)], tok_s, tok_r.at[h], sibling
            ).wait_recv()
        for h in range(2):
            xt[h] = slab[h].reshape(512, 256).T

    first = jnp.where(l < 2, 3, 1)
    second = 4 - first

    def ref(s):
        tt = (t + s) % 4
        sibling_chunks(tt, 0)
        ref_part(tt)

    def gt_cols(h):
        return pl.ds(pl.multiple_of(slice_cols + h * 1024, 256), 256)

    gt_own = [pltpu.make_async_copy(gt_send.at[h, me], gt_out.at[:, gt_cols(h)], load_s.at[h]) for h in range(2)]

    def grad_tokens():
        for tt in range(4):
            sibling_chunks(tt, 2)

        @pl.loop(0, 2)
        def _(j):
            rows = [gk[tt, pl.ds(j * 8, 8)].reshape(256, 256) for tt in range(4)]
            for h in range(2):
                acc = jnp.zeros((256, 256), F32)
                for tt in range(4):
                    acc = acc + lax.dot_general(
                        rows[tt], policy_of(h, tt), (((1,), (1,)), ((), ())), preferred_element_type=F32
                    )
                gt_send[h, pl.ds(j * 8, 8)] = acc.astype(BF16).reshape(8, 32, 256)

    def gt_sends():
        @pl.loop(1, 16)
        def _(s):
            k = (me + s) % 16
            for h in range(2):
                remote(gt_send.at[h, k], gt_out.at[:, gt_cols(h)], gt_s, gt_r, plane(k // 4, k % 4)).start()

        for copy in gt_own:
            copy.start()

    gk_second(t)
    tick(0)
    heard_near()
    gk_send(2)
    gk_exchanged(1)
    gk_exchanged(3)
    tick(2)
    tick(4)
    tick(5)
    gk_second((t + 3) % 4)
    gk_second((t + 1) % 4)
    gk_exchanged(2)
    tick(7)
    tokens_done()
    tick(8)
    tick(9)
    gw_part(0)
    tick(10)
    ref(0)
    tick(12)
    tick(13)
    gw_part(3)
    gw_first(t)
    tick(14)
    gw_part(1)
    tick(15)
    gw_part(2)
    gw_first((t + 3) % 4)
    tick(17)
    gw_first((t + 1) % 4)
    ref(first)
    gw_first((t + 2) % 4)
    ref_second(t)
    tick(18)
    tick(19)
    ref(second)
    ref_second((t + first) % 4)
    gw_second(t)
    gw_second((t + 2) % 4)
    gw_second((t + 3) % 4)
    gw_second((t + 1) % 4)
    tick(22)
    tick(23)
    ref(2)
    ref_second((t + second) % 4)
    heard_far()
    tick(28)
    gw_third(t)
    gw_third((t + 3) % 4)
    gw_third((t + 1) % 4)
    gw_third((t + 2) % 4)
    grad_tokens()
    ref_second((t + 2) % 4)
    ref_third(0)
    ref_third(first)
    gt_sends()
    ref_third(second)
    ref_third(2)

    src_self = (2 * (l % 2) + x // 2 == y) & (y * 2 + l // 2 == i)
    total = jnp.zeros((64, 256), F32)
    for slot in range(5):
        def arrived():
            remote(gw_fin.at[slot], gw_fin.at[slot], gw_s.at[0, 0, 0], fin_r.at[slot], sibling).wait_recv()

        if slot == 0:
            pl.when(jnp.logical_not(src_self))(arrived)
        else:
            arrived()
        total = total + gw_fin[slot].astype(F32)
    gw_out[...] = total * lax.rsqrt(jnp.full((1, 1), 16384.0, F32))

    for copy in gt_own:
        copy.wait()
    gt_all = gt_out.at[:, pl.ds(0, 30 * 256)]
    remote(gt_all, gt_all, gt_s, gt_r, sibling).wait_recv()
    remote(keys_out.at[pl.ds(0, 96)], keys_out.at[pl.ds(0, 96)], kz_s, kz_r, sibling).wait()
    remote(gkeys_v.at[pl.ds(0, 96)], gkeys_v.at[pl.ds(0, 96)], gkz_s, gkz_r.at[0], sibling).wait_send()
    remote(gt_all, gt_all, tok_s, tok_r.at[0], sibling).wait_send()
    remote(gt_all, gt_all, gt_s, gt_r, sibling).wait_send()
    remote(gk.at[0, pl.ds(0, 9)], gk.at[0, pl.ds(0, 9)], gk1_s, gk1_r.at[0, 0], sibling).wait_send()
    remote(gk.at[0, pl.ds(0, 15)], gk.at[0, pl.ds(0, 15)], gkd_s, gkd_r, sibling).wait_send()
    remote(rs1.at[pl.ds(0, 3)], rs1.at[pl.ds(0, 3)], gk2_s, gk2_r.at[0, 0], sibling).wait_send()
    remote(part.at[pl.ds(0, 3)], part.at[pl.ds(0, 3)], rs1_s, rs1_r.at[0, 0], sibling).wait_send()
    remote(rs2, rs2, rs2_s, rs2_r.at[0, 0], sibling).wait_send()
    for dirn, steps in ((0, l), (1, 3 - l)):
        for sent, here in ((4, steps == 3), (8, steps == 0), (6, among(steps, 1, 2))):
            @pl.when(here)
            def _():
                rows = cw.at[pl.ds(0, sent)]
                remote(rows, rows, cw_s.at[dirn], cw_r.at[dirn, 0], sibling).wait_send()
    remote(cw.at[pl.ds(0, 16)], cw.at[pl.ds(0, 16)], cws_s, cws_r.at[0], sibling).wait_send()
    remote(gwx_send, gwx_send, gwx_s, gwx_r.at[0], sibling).wait_send()
    for tt in range(4):
        for q in range(2):
            final = is_final(tree_place(tt, q))

            @pl.when(jnp.logical_not(final))
            def _():
                remote(gw_send.at[tt, q], gw_send.at[tt, q], gw_s.at[tt, q, 2], gwa_r.at[tt, q], sibling).wait_send()

            for e in range(2):
                rows = gw_send.at[tt, q, pl.ds(e * 64, 64)]

                @pl.when(final & jnp.logical_not(is_self(tt, 2 * q + e)))
                def _():
                    remote(rows, rows, gw_s.at[tt, q, e], gwa_r.at[tt, q], sibling).wait_send()


def body(tokens, ref_codes, ref_scales, policy_weight, grad_keys):
    vmem = pl.BlockSpec(memory_space=pltpu.VMEM)
    hbm = pl.BlockSpec(memory_space=pltpu.HBM)
    dma = pltpu.SemaphoreType.DMA
    return pl.pallas_call(
        kernel,
        out_shape=(
            jax.ShapeDtypeStruct((128, 256), BF16),
            jax.ShapeDtypeStruct((64, 256), F32),
            jax.ShapeDtypeStruct((32, 8192), BF16),
        ),
        in_specs=[hbm] * 5,
        out_specs=[vmem, vmem, hbm],
        scratch_shapes=[
            pltpu.VMEM((2, 128, 256), BF16),
            pltpu.VMEM((8, 256), F32),
            pltpu.VMEM((128, 256), BF16),
            pltpu.VMEM((2, 16, 32, 256), BF16),
            pltpu.VMEM((4, 16, 32, 256), BF16),
            pltpu.VMEM((32, 128, 256), BF16),
            pltpu.VMEM((2, 256, 512), BF16),
            pltpu.VMEM((4, 16, 32, 256), BF16),
            pltpu.VMEM((4, 3, 4, 32, 256), BF16),
            pltpu.VMEM((4, 4, 32, 256), BF16),
            pltpu.VMEM((4, 3, 32, 256), BF16),
            pltpu.VMEM((4, 32, 256), BF16),
            pltpu.VMEM((4, 2, 128, 256), BF16),
            pltpu.VMEM((4, 2, 128, 256), BF16),
            pltpu.VMEM((4, 2, 128, 256), F32),
            pltpu.VMEM((4, 2, 128, 256), BF16),
            pltpu.VMEM((4, 2, 128, 256), BF16),
            pltpu.VMEM((4, 2, 128, 256), BF16),
            pltpu.VMEM((5, 64, 256), BF16),
            pltpu.VMEM((2, 16, 32, 256), BF16),
            dma((7,)),
            dma, dma((2,)),
            dma, dma((4,)),
            dma, dma((4, 4)), dma, dma((4, 4)), dma, dma,
            dma((2,)), dma((2, 6)), dma, dma((16,)),
            dma, dma((4, 4)), dma, dma((4, 4)),
            dma, dma,
            dma, dma((4,)),
            dma((4, 2, 3)), dma((4, 2)), dma((4, 2)), dma((5,)),
            dma, dma,
            pltpu.SemaphoreType.REGULAR, pltpu.SemaphoreType.REGULAR,
        ],
        compiler_params=pltpu.CompilerParams(
            collective_id=0, has_side_effects=True, vmem_limit_bytes=64 * 1024 * 1024 - 256 * 1024
        ),
        cost_estimate=pl.CostEstimate(flops=1_700_000_000, bytes_accessed=4_000_000, transcendentals=0),
    )(tokens, ref_codes, ref_scales, policy_weight, grad_keys)


def solution(mesh):
    return jax.shard_map(
        body,
        mesh=mesh,
        in_specs=(
            P(("outer", "inner", "tensor"), None),
            P("inner", None, "tensor"),
            P("inner", "tensor"),
            P("inner", "tensor"),
            P(("outer", "inner"), "tensor"),
        ),
        out_specs=(
            P(("outer", "inner"), "tensor"),
            P(("outer", "inner"), "tensor"),
            P(("outer", "inner", "tensor"), None),
        ),
        check_vma=False,
    )
```

time: 84.9 us -> 74.3 us (0.88)
  the two profiles are of different devices: /device:TPU:39 before, /device:TPU:3 now
where the time goes in v3:
time: 74.3 us; the launch traced here: 74 us
  Pallas kernels  69.4 us (93%)
  local copies, waits for them, and re-layouts  4.01 us (5%)
    pallas_call x1, Pallas kernels, body(): pl.pallas_call(kernel, out_shape=(jax.ShapeDtypeStruct((128, 256), BF16),...  69.4 us
    unnamed x5, local copies, waits for them, and re-layouts  4.01 us

profile of v3, /device:TPU:3, one launch (start us, length us, event | category | flops | bytes accessed | tf_op | source)
XLA Modules:
  0.0 74.0 jit_solution(805563348510438942)
XLA Ops:
  0.6 69.4 %shard_map.76 = (bf16[128,256]{1,0:T(8,128)(2,1)}, f32[64,256]{1,0:T(8,128)}, bf16[32,8192]{1,0:T(8,128)(2,1)}) custom-call(bf16[32,8192]{1,0:T(8,128)(2,1)} %tok.1, bf16[8,128,256]{2,1,0:T(8,128)(2,1)} %codes.1, f32[8,256]{1,0:T(8,128)} %scales.1, bf16[1024,256]{1,0:T(8,128)(2,1)} %policy.1, bf16[128,256]{1,0:T(8,128)(2,1)} %gkeys.1), custom_call_target="tpu_custom_call" | custom-call | flops 1700000000 | bytes 4000000 | tf_op jit(solution)/shard_map/pallas_call | solution.py:519
  70.0 0.0 copy-start
  70.0 1.5 %copy.11 = bf16[128,256]{1,0:T(8,128)(2,1)} copy(bf16[128,256]{1,0:T(8,128)(2,1)} %get-tuple-element.6) | data formatting | bytes 131072
  71.5 0.0 copy-done
  71.5 0.6 copy.12
  72.2 1.9 %copy.13 = bf16[32,8192]{1,0:T(8,128)(2,1)} copy(bf16[32,8192]{1,0:T(8,128)(2,1)} %get-tuple-element.8) | data formatting | bytes 1048576
Async XLA Ops:
  70.0 1.5 %copy-start = (f32[64,256]{1,0:T(8,128)S(1)}, f32[64,256]{1,0:T(8,128)}, u32[]{:S(2)}) copy-start(f32[64,256]{1,0:T(8,128)} %get-tuple-element.7) | copy-start | bytes 196612

commit v4 on v3

--- a/solution.py
+++ b/solution.py
@@ -39,7 +39,7 @@
     gwx_send, gwx_recv, gwp, gw_send, gw_a, gw_b, gw_fin, gt_send,
     load_s, tok_s, tok_r, gkz_s, gkz_r, gk1_s, gk1_r, gk2_s, gk2_r, gkd_s, gkd_r, cw_s, cw_r, cws_s, cws_r,
     rs1_s, rs1_r, rs2_s, rs2_r, kz_s, kz_r, gwx_s, gwx_r, gw_s, gwa_r, gwb_r, fin_r, gt_s, gt_r,
-    near_in, far_in,
+    near_in, far_in, gk_relay, relay_s, relay_r, passed_r,
 ):
     o = lax.axis_index("outer")
     i = lax.axis_index("inner")
@@ -159,6 +159,22 @@
     gk_send(1)
     gk_send(3)
 
+    def relay_rows(n):
+        return pl.ds(pl.multiple_of((t + 2) % 4 * 32 + n * 16, 16), 16)
+
+    for n, s in ((0, 1), (1, 3)):
+        remote(gkeys_v.at[relay_rows(n)], gk_relay.at[n], gkz_s, relay_r.at[n], (o, i, (t + s) % 4)).start()
+
+    def gk_landing(tt, n):
+        return gk.at[tt, me, pl.ds(n * 16, 16)]
+
+    def gk_passed_on():
+        for n, s in ((0, 1), (1, 3)):
+            remote(gk_relay.at[n], gk_relay.at[n], gkz_s, relay_r.at[n], sibling).wait_recv()
+            remote(
+                gk_relay.at[n], gk_landing((t + 4 - s) % 4, n), relay_s, passed_r.at[n], (o, i, (t + s) % 4)
+            ).start()
+
     def gk_first(tt):
         for s in range(1, 4):
             remote(gk.at[tt, me], gk.at[tt, me], gk1_s, gk1_r.at[tt, s], plane(a, (b + s) % 4)).start()
@@ -188,10 +204,12 @@
 
     def gk_exchanged(s):
         tt = (t + 4 - s) % 4
-        remote(gk.at[tt, me], gk.at[tt, me], gkz_s, gkz_r.at[s], sibling).wait_recv()
         if s == 2:
+            for n in range(2):
+                remote(gk_landing(tt, n), gk_landing(tt, n), gkz_s, passed_r.at[n], sibling).wait_recv()
             gk_direct(tt)
         else:
+            remote(gk.at[tt, me], gk.at[tt, me], gkz_s, gkz_r.at[s], sibling).wait_recv()
             gk_first(tt)
 
     gk_first(t)
@@ -373,50 +391,55 @@
         sibling_chunks(tt, 0)
         ref_part(tt)
 
-    def gt_cols(h):
-        return pl.ds(pl.multiple_of(slice_cols + h * 1024, 256), 256)
-
-    gt_own = [pltpu.make_async_copy(gt_send.at[h, me], gt_out.at[:, gt_cols(h)], load_s.at[h]) for h in range(2)]
-
-    def grad_tokens():
+    def gt_cols(h, q):
+        return pl.ds(pl.multiple_of(slice_cols + h * 1024 + q * 128, 128), 128)
+
+    half = jnp.where(l < 2, 0, 1)
+
+    def grad_tokens(q):
         for tt in range(4):
-            sibling_chunks(tt, 2)
+            cw_sibling((1 - c) * 16 + tt * 4 + 2 + q).wait_recv()
 
         @pl.loop(0, 2)
         def _(j):
-            rows = [gk[tt, pl.ds(j * 8, 8)].reshape(256, 256) for tt in range(4)]
+            acc = jnp.zeros((256, 256), F32)
+            for tt in range(4):
+                w = jnp.concatenate([cw[tt * 4 + 2 + q], cw[16 + tt * 4 + 2 + q]], axis=0)
+                g = gk[tt, pl.ds(j * 8, 8)].reshape(256, 256)
+                acc = acc + lax.dot_general(g, w, (((1,), (1,)), ((), ())), preferred_element_type=F32)
+            out = acc.astype(BF16)
             for h in range(2):
-                acc = jnp.zeros((256, 256), F32)
-                for tt in range(4):
-                    acc = acc + lax.dot_general(
-                        rows[tt], policy_of(h, tt), (((1,), (1,)), ((), ())), preferred_element_type=F32
-                    )
-                gt_send[h, pl.ds(j * 8, 8)] = acc.astype(BF16).reshape(8, 32, 256)
-
-    def gt_sends():
+                gt_send[q, h, pl.ds(j * 8, 8)] = out[:, h * 128 : (h + 1) * 128].reshape(8, 32, 128)
+
+    def gt_own(n, q, h):
+        return pltpu.make_async_copy(gt_send.at[q, h, me], gt_out.at[:, gt_cols(h, q)], load_s.at[2 * n + h])
+
+    def gt_sends(n, q):
         @pl.loop(1, 16)
         def _(s):
             k = (me + s) % 16
             for h in range(2):
-                remote(gt_send.at[h, k], gt_out.at[:, gt_cols(h)], gt_s, gt_r, plane(k // 4, k % 4)).start()
-
-        for copy in gt_own:
-            copy.start()
+                remote(
+                    gt_send.at[q, h, k], gt_out.at[:, gt_cols(h, q)], gt_s, gt_r, plane(k // 4, k % 4)
+                ).start()
+
+        for h in range(2):
+            gt_own(n, q, h).start()
 
     gk_second(t)
     tick(0)
     heard_near()
-    gk_send(2)
     gk_exchanged(1)
     gk_exchanged(3)
+    gk_passed_on()
     tick(2)
     tick(4)
     tick(5)
     gk_second((t + 3) % 4)
     gk_second((t + 1) % 4)
-    gk_exchanged(2)
     tick(7)
     tokens_done()
+    gk_exchanged(2)
     tick(8)
     tick(9)
     gw_part(0)
@@ -434,31 +457,33 @@
     tick(17)
     gw_first((t + 1) % 4)
     ref(first)
+    tick(18)
     gw_first((t + 2) % 4)
+    tick(19)
     ref_second(t)
-    tick(18)
-    tick(19)
     ref(second)
-    ref_second((t + first) % 4)
-    gw_second(t)
-    gw_second((t + 2) % 4)
-    gw_second((t + 3) % 4)
-    gw_second((t + 1) % 4)
     tick(22)
     tick(23)
     ref(2)
+    ref_second((t + first) % 4)
+    gw_second(t)
+    gw_second((t + 3) % 4)
+    gw_second((t + 1) % 4)
+    gw_second((t + 2) % 4)
+    grad_tokens(half)
+    gt_sends(0, half)
     ref_second((t + second) % 4)
+    ref_third(0)
+    ref_third(first)
     heard_far()
     tick(28)
+    grad_tokens(1 - half)
+    ref_second((t + 2) % 4)
+    gt_sends(1, 1 - half)
     gw_third(t)
     gw_third((t + 3) % 4)
     gw_third((t + 1) % 4)
     gw_third((t + 2) % 4)
-    grad_tokens()
-    ref_second((t + 2) % 4)
-    ref_third(0)
-    ref_third(first)
-    gt_sends()
     ref_third(second)
     ref_third(2)
 
@@ -475,11 +500,13 @@
         total = total + gw_fin[slot].astype(F32)
     gw_out[...] = total * lax.rsqrt(jnp.full((1, 1), 16384.0, F32))
 
-    for copy in gt_own:
-        copy.wait()
+    for n, q in ((0, half), (1, 1 - half)):
+        for h in range(2):
+            gt_own(n, q, h).wait()
     gt_all = gt_out.at[:, pl.ds(0, 30 * 256)]
     remote(gt_all, gt_all, gt_s, gt_r, sibling).wait_recv()
     remote(keys_out.at[pl.ds(0, 96)], keys_out.at[pl.ds(0, 96)], kz_s, kz_r, sibling).wait()
+    remote(gk_relay, gk_relay, relay_s, relay_r.at[0], sibling).wait_send()
     remote(gkeys_v.at[pl.ds(0, 96)], gkeys_v.at[pl.ds(0, 96)], gkz_s, gkz_r.at[0], sibling).wait_send()
     remote(gt_all, gt_all, tok_s, tok_r.at[0], sibling).wait_send()
     remote(gt_all, gt_all, gt_s, gt_r, sibling).wait_send()
@@ -512,11 +539,24 @@
                     remote(rows, rows, gw_s.at[tt, q, e], gwa_r.at[tt, q], sibling).wait_send()
 
 
+def copy_kernel(keys, gw, gt, keys_out, gw_out, gt_out, keys_v, gw_v, gt_v, in_s, out_s):
+    rows = ((gt, gt_v, gt_out), (keys, keys_v, keys_out), (gw, gw_v, gw_out))
+    loads = [pltpu.make_async_copy(src, mid, in_s.at[n]) for n, (src, mid, _) in enumerate(rows)]
+    stores = [pltpu.make_async_copy(mid, dst, out_s.at[n]) for n, (_, mid, dst) in enumerate(rows)]
+    for load in loads:
+        load.start()
+    for load, store in zip(loads, stores):
+        load.wait()
+        store.start()
+    for store in stores:
+        store.wait()
+
+
 def body(tokens, ref_codes, ref_scales, policy_weight, grad_keys):
     vmem = pl.BlockSpec(memory_space=pltpu.VMEM)
     hbm = pl.BlockSpec(memory_space=pltpu.HBM)
     dma = pltpu.SemaphoreType.DMA
-    return pl.pallas_call(
+    outs = pl.pallas_call(
         kernel,
         out_shape=(
             jax.ShapeDtypeStruct((128, 256), BF16),
@@ -545,7 +585,7 @@
             pltpu.VMEM((4, 2, 128, 256), BF16),
             pltpu.VMEM((4, 2, 128, 256), BF16),
             pltpu.VMEM((5, 64, 256), BF16),
-            pltpu.VMEM((2, 16, 32, 256), BF16),
+            pltpu.VMEM((2, 2, 16, 32, 128), BF16),
             dma((7,)),
             dma, dma((2,)),
             dma, dma((4,)),
@@ -557,12 +597,22 @@
             dma((4, 2, 3)), dma((4, 2)), dma((4, 2)), dma((5,)),
             dma, dma,
             pltpu.SemaphoreType.REGULAR, pltpu.SemaphoreType.REGULAR,
+            pltpu.VMEM((2, 16, 256), BF16),
+            dma, dma((2,)), dma((2,)),
         ],
         compiler_params=pltpu.CompilerParams(
             collective_id=0, has_side_effects=True, vmem_limit_bytes=64 * 1024 * 1024 - 256 * 1024
         ),
         cost_estimate=pl.CostEstimate(flops=1_700_000_000, bytes_accessed=4_000_000, transcendentals=0),
     )(tokens, ref_codes, ref_scales, policy_weight, grad_keys)
+    return pl.pallas_call(
+        copy_kernel,
+        out_shape=tuple(jax.ShapeDtypeStruct(out.shape, out.dtype) for out in outs),
+        in_specs=[hbm] * 3,
+        out_specs=[hbm] * 3,
+        scratch_shapes=[pltpu.VMEM(out.shape, out.dtype) for out in outs] + [dma((3,)), dma((3,))],
+        compiler_params=pltpu.CompilerParams(vmem_limit_bytes=62 * 1024 * 1024),
+    )(*outs)
 
 
 def solution(mesh):

time: 74.3 us -> 67.1 us (0.903)
  the two profiles are of different devices: /device:TPU:3 before, /device:TPU:1 now
where the time goes in v4:
time: 67.1 us; the launch traced here: 66.1 us
  Pallas kernels  65.5 us (98%)
    pallas_call x1, Pallas kernels, body(): pl.pallas_call(kernel, out_shape=(jax.ShapeDtypeStruct((128, 256), BF16),...  63.6 us
    pallas_call x1, Pallas kernels, body(): pl.pallas_call(copy_kernel, out_shape=tuple((jax.ShapeDtypeStruct(out.sha...  1.92 us

profile of v4, /device:TPU:1, one launch (start us, length us, event | category | flops | bytes accessed | tf_op | source)
XLA Modules:
  0.0 66.1 jit_solution(3821256287411014143)
XLA Ops:
  0.6 63.6 %shard_map.76 = (bf16[128,256]{1,0:T(8,128)(2,1)}, f32[64,256]{1,0:T(8,128)}, bf16[32,8192]{1,0:T(8,128)(2,1)}) custom-call(bf16[32,8192]{1,0:T(8,128)(2,1)} %tok.1, bf16[8,128,256]{2,1,0:T(8,128)(2,1)} %codes.1, f32[8,256]{1,0:T(8,128)} %scales.1, bf16[1024,256]{1,0:T(8,128)(2,1)} %policy.1, bf16[128,256]{1,0:T(8,128)(2,1)} %gkeys.1), custom_call_target="tpu_custom_call" | custom-call | flops 1700000000 | bytes 4000000 | tf_op jit(solution)/shard_map/pallas_call | solution.py:559
  64.2 1.9 %shard_map.77 = (bf16[128,256]{1,0:T(8,128)(2,1)}, f32[64,256]{1,0:T(8,128)}, bf16[32,8192]{1,0:T(8,128)(2,1)}) custom-call(bf16[128,256]{1,0:T(8,128)(2,1)} %get-tuple-element.6.keys, f32[64,256]{1,0:T(8,128)} %get-tuple-element.7.gw, bf16[32,8192]{1,0:T(8,128)(2,1)} %get-tuple-element.8.gt), custom_call_target="tpu_custom_call" | custom-call | tf_op jit(solution)/shard_map/pallas_call | solution.py:608

commit v5 on v4

--- a/solution.py
+++ b/solution.py
@@ -478,8 +478,8 @@
     heard_far()
     tick(28)
     grad_tokens(1 - half)
+    gt_sends(1, 1 - half)
     ref_second((t + 2) % 4)
-    gt_sends(1, 1 - half)
     gw_third(t)
     gw_third((t + 3) % 4)
     gw_third((t + 1) % 4)

time: 67.1 us -> 71.3 us (1.063)
  Pallas kernels: 65.5 us -> 70.4 us
    pallas_call x1, Pallas kernels: 63.6 us -> 68.4 us  [body(): pl.pallas_call(kernel, out_shape=(jax.ShapeDtypeStruct((128, 256), BF16),...]
where the time goes in v5:
time: 71.3 us; the launch traced here: 71 us
  Pallas kernels  70.4 us (99%)
    pallas_call x1, Pallas kernels, body(): pl.pallas_call(kernel, out_shape=(jax.ShapeDtypeStruct((128, 256), BF16),...  68.4 us
    pallas_call x1, Pallas kernels, body(): pl.pallas_call(copy_kernel, out_shape=tuple((jax.ShapeDtypeStruct(out.sha...  1.92 us

profile of v5, /device:TPU:1, one launch (start us, length us, event | category | flops | bytes accessed | tf_op | source)
XLA Modules:
  0.0 71.0 jit_solution(527613593672174830)
XLA Ops:
  0.6 68.4 %shard_map.76 = (bf16[128,256]{1,0:T(8,128)(2,1)}, f32[64,256]{1,0:T(8,128)}, bf16[32,8192]{1,0:T(8,128)(2,1)}) custom-call(bf16[32,8192]{1,0:T(8,128)(2,1)} %tok.1, bf16[8,128,256]{2,1,0:T(8,128)(2,1)} %codes.1, f32[8,256]{1,0:T(8,128)} %scales.1, bf16[1024,256]{1,0:T(8,128)(2,1)} %policy.1, bf16[128,256]{1,0:T(8,128)(2,1)} %gkeys.1), custom_call_target="tpu_custom_call" | custom-call | flops 1700000000 | bytes 4000000 | tf_op jit(solution)/shard_map/pallas_call | solution.py:559
  69.1 1.9 %shard_map.77 = (bf16[128,256]{1,0:T(8,128)(2,1)}, f32[64,256]{1,0:T(8,128)}, bf16[32,8192]{1,0:T(8,128)(2,1)}) custom-call(bf16[128,256]{1,0:T(8,128)(2,1)} %get-tuple-element.6.keys, f32[64,256]{1,0:T(8,128)} %get-tuple-element.7.gw, bf16[32,8192]{1,0:T(8,128)(2,1)} %get-tuple-element.8.gt), custom_call_target="tpu_custom_call" | custom-call | tf_op jit(solution)/shard_map/pallas_call | solution.py:608
